TPU v7x, 32 devices: a whole 2x2x4 slice. The times are simulated.
32 devices in a mesh: groups: 2 (over x), context: 8 (over z, y), dp: 2 (over core).
Axes of the slice: x: 2, y: 2, z: 4, core: 2. Of those that a mesh axis runs over, the one named last changes fastest.
Arguments:
- hyena_input: bfloat16 [4, 1024, 512], P(('groups', 'dp'), 'context'), parts along dimension 0, may hold values from -6 to 6
- gate_input: bfloat16 [4, 1024, 512], P(('groups', 'dp'), 'context'), parts along dimension 0, may hold values from -6 to 6
- filter_taps: float32 [1024, 1024], P('context', 'groups'), parts along dimension 1, may hold values from -2.5 to 2.5
- cotangent: bfloat16 [4, 1024, 512], P(('groups', 'dp'), 'context'), parts along dimension 0, may hold values from -6 to 6
Outputs:
- gated: bfloat16 [4, 1024, 512], P(('groups', 'dp'), 'context'), parts along dimension 0
- gate_grad: bfloat16 [4, 1024, 512], P(('groups', 'dp'), 'context'), parts along dimension 0
- input_grad: bfloat16 [4, 1024, 512], P(('groups', 'dp'), 'context'), parts along dimension 0
- filter_grad: float32 [1024, 1024], P('context', ('groups', 'dp')), parts along dimension 1
There are 2 independent parts, one for each index of `groups`. A program takes and returns all parts, laid end to end along the dimension named above; each array names one. Nothing has to cross between parts.
All inputs are finite; a program needn't handle non-finite values.
Results may differ from a plain program's by a relative error of at most 0.001.
Values sent between devices are 32-bit elements; how exact they have to be, the bound alone decides.
No kernel may reach another device: no remote copies, remote signals or barrier semaphores. Data moves between devices by JAX's collectives and lax.ppermute only.
A program may use at most 64 MiB of HBM per device.

v0:
```python
import functools
import math

import jax
import jax.numpy as jnp
import ml_dtypes
import numpy as np
from jax import lax
from jax.experimental import pallas as pl
from jax.experimental.pallas import tpu as pltpu
from jax.sharding import PartitionSpec as P

LANES = 128
HIGHEST = lax.Precision.HIGHEST


def block_table(rows):
    index = np.arange(rows)
    angle = 2.0 * np.pi * (np.outer(index, index) % rows) / rows
    cosine, sine = np.cos(angle), np.sin(angle)
    return np.block([[cosine, -sine], [sine, cosine]])


def residue_table(count, rows):
    angle = 2.0 * np.pi * np.outer(np.arange(count), np.arange(rows)) / (2 * (count - 1) * rows)
    return np.cos(angle), np.sin(angle)


def two_halves(table):
    high = table.astype(np.float32).astype(ml_dtypes.bfloat16)
    low = (table - high.astype(np.float64)).astype(np.float32).astype(ml_dtypes.bfloat16)
    return high, low


def split(value):
    high = value.astype(jnp.bfloat16)
    return high, (value - high.astype(jnp.float32)).astype(jnp.bfloat16)


def dot3(value, high_ref, low_ref):
    high, low = split(value)
    dot = functools.partial(jnp.dot, preferred_element_type=jnp.float32)
    return dot(high, high_ref[...]) + (dot(low, high_ref[...]) + dot(high, low_ref[...]))


def weighted(terms):
    total = None
    for weight, value in terms:
        if abs(weight) < 1e-12:
            continue
        if abs(weight - 1.0) < 1e-12:
            part = value
        elif abs(weight + 1.0) < 1e-12:
            total = -value if total is None else total - value
            continue
        else:
            part = value * np.float32(weight)
        total = part if total is None else total + part
    return total


def add(first, second):
    if first is None or second is None:
        return second if first is None else first
    return first + second


def sub(first, second):
    if second is None:
        return first
    return -second if first is None else first - second


def columns_of(arrived_ref, block, seqs, half):
    width = seqs * half
    at = lambda seq, first, count: arrived_ref[block * seqs + seq, pl.ds(first, count), :]
    parts = [at(seq, 0, width) for seq in range(seqs)]
    parts += [at(seq, width, width) for seq in range(seqs)]
    parts += [at(seq, 2 * width, half) for seq in range(seqs)]
    return jnp.concatenate(parts, axis=0)


def core_kernel(blocks, seqs, half, scale, arrived_ref, high_ref, low_ref, cos_ref, sin_ref, leave_ref, real_ref, imag_ref):
    width = seqs * half
    cells = 2 * blocks
    turn = 2.0 * math.pi / cells
    sums = {}
    columns = [columns_of(arrived_ref, block, seqs, half) for block in range(blocks)]
    for k in range(blocks // 2 + 1):
        even = range(0, blocks, 2)
        odd = range(1, blocks, 2)
        cos_even = weighted([(math.cos(turn * k * p), columns[p]) for p in even])
        cos_odd = weighted([(math.cos(turn * k * p), columns[p]) for p in odd])
        sin_even = weighted([(math.sin(turn * k * p), columns[p]) for p in even])
        sin_odd = weighted([(math.sin(turn * k * p), columns[p]) for p in odd])
        sums[k] = (add(cos_even, cos_odd), sub(sub(None, sin_even), sin_odd))
        if k != blocks - k:
            sums[blocks - k] = (sub(cos_even, cos_odd), sub(sin_even, sin_odd))
    for k in range(blocks + 1):
        real, imag = sums[k]
        if k > 0:
            cosine, sine = cos_ref[pl.ds(k, 1), :], sin_ref[pl.ds(k, 1), :]
            if imag is None:
                real, imag = real * cosine, -real * sine
            else:
                real, imag = real * cosine + imag * sine, imag * cosine - real * sine
        if imag is None:
            imag = jnp.zeros_like(real)
        spec = dot3(jnp.concatenate([real, imag], axis=1), high_ref, low_ref)
        spec_re, spec_im = spec[:, :LANES], spec[:, LANES:]
        part = lambda value, first, count: value[first : first + count]
        taps_re, taps_im = part(spec_re, 2 * seqs * width, width), part(spec_im, 2 * seqs * width, width)
        outs, grads = [], []
        filt_re = filt_im = None
        for seq in range(seqs):
            x_re, x_im = part(spec_re, seq * width, width), part(spec_im, seq * width, width)
            c_re, c_im = (part(value, (seqs + seq) * width, width) for value in (spec_re, spec_im))
            outs.append((x_re * taps_re - x_im * taps_im, x_re * taps_im + x_im * taps_re))
            grads.append((c_re * taps_re + c_im * taps_im, c_im * taps_re - c_re * taps_im))
            filt_re = add(filt_re, c_re * x_re + c_im * x_im)
            filt_im = add(filt_im, c_im * x_re - c_re * x_im)
        products = outs + grads + [(filt_re * scale, filt_im * scale)]
        real = jnp.concatenate([product[0] for product in products], axis=0)
        imag = jnp.concatenate([product[1] for product in products], axis=0)
        back = dot3(jnp.concatenate([real, -imag], axis=1), high_ref, low_ref)
        real, imag = back[:, :LANES], -back[:, LANES:]
        if k > 0:
            cosine, sine = cos_ref[pl.ds(k, 1), :], sin_ref[pl.ds(k, 1), :]
            if k < blocks:
                imag_ref[k] = imag * cosine + real * sine
            real = real * cosine - imag * sine
        real_ref[k] = real
    inverse = 1.0 / (cells * LANES)
    for first in range(0, (2 * seqs + 1) * seqs * half, 8):
        rows = pl.ds(first, 8)
        real = [real_ref[k, rows, :] * np.float32(inverse if k in (0, blocks) else 2.0 * inverse) for k in range(blocks + 1)]
        imag = [None] + [imag_ref[k, rows, :] * np.float32(2.0 * inverse) for k in range(1, blocks)] + [None]
        for block in range(blocks // 2 + 1):
            cos_even = weighted([(math.cos(turn * k * block), real[k]) for k in range(0, blocks + 1, 2)])
            cos_odd = weighted([(math.cos(turn * k * block), real[k]) for k in range(1, blocks, 2)])
            sin_even = weighted([(math.sin(turn * k * block), imag[k]) for k in range(2, blocks, 2)])
            sin_odd = weighted([(math.sin(turn * k * block), imag[k]) for k in range(1, blocks, 2)])
            put(leave_ref, block, first, sub(sub(add(cos_even, cos_odd), sin_even), sin_odd), seqs, half)
            if block not in (0, blocks - block):
                put(leave_ref, blocks - block, first, sub(add(sub(cos_even, cos_odd), sin_even), sin_odd), seqs, half)


def put(leave_ref, block, first, value, seqs, half):
    width = seqs * half
    if first < 2 * seqs * width:
        seq, row = first // width % seqs, first // width // seqs * width + first % width
    else:
        seq, row = (first - 2 * seqs * width) // half, 2 * width + (first - 2 * seqs * width) % half
    leave_ref[block * seqs + seq, pl.ds(row, 8), :] = value


def core(arrived, blocks, seqs, half, scale):
    high, low = two_halves(block_table(LANES))
    cosine, sine = residue_table(blocks + 1, LANES)
    rows = (2 * seqs + 1) * seqs * half
    vmem = pl.BlockSpec(memory_space=pltpu.VMEM)
    return pl.pallas_call(
        functools.partial(core_kernel, blocks, seqs, half, np.float32(scale)),
        out_shape=jax.ShapeDtypeStruct(arrived.shape, jnp.float32),
        in_specs=[vmem] * 5,
        out_specs=vmem,
        scratch_shapes=[pltpu.VMEM((blocks + 1, rows, LANES), jnp.float32)] * 2,
        compiler_params=pltpu.CompilerParams(vmem_limit_bytes=40 * 2**20),
        name="core",
    )(arrived, jnp.asarray(high), jnp.asarray(low), jnp.asarray(cosine, jnp.float32), jnp.asarray(sine, jnp.float32))


def pack_kernel(seqs, half, signal_ref, gate_ref, taps_ref, upstream_ref, leave_ref):
    width = seqs * half
    channels = signal_ref.shape[1]
    group = LANES // half
    per_half = channels // seqs // LANES
    for tile in range(channels // LANES):
        lanes = pl.ds(tile * LANES, LANES)
        where, to = tile // per_half, pl.ds(tile % per_half * group, group)
        signal = signal_ref[:, lanes].astype(jnp.float32)
        carried = upstream_ref[:, lanes].astype(jnp.float32) * gate_ref[:, lanes].astype(jnp.float32)
        leave_ref[to, pl.ds(where * half, half), :] = signal.T.reshape(group, half, LANES)
        leave_ref[to, pl.ds(width + where * half, half), :] = carried.T.reshape(group, half, LANES)
    own = lax.axis_index("dp")
    for tile in range(per_half):
        lanes = pl.ds(pl.multiple_of((own * per_half + tile) * LANES, LANES), LANES)
        leave_ref[pl.ds(tile * group, group), pl.ds(2 * width, half), :] = taps_ref[:, lanes].T.reshape(group, half, LANES)


def unpack_kernel(seqs, half, arrived_ref, gate_ref, upstream_ref, gated_ref, gate_grad_ref, input_grad_ref, filter_grad_ref):
    width = seqs * half
    channels = gate_ref.shape[1]
    group = LANES // half
    per_half = channels // seqs // LANES
    for tile in range(channels // LANES):
        lanes = pl.ds(tile * LANES, LANES)
        where, of = tile // per_half, pl.ds(tile % per_half * group, group)
        convolved = arrived_ref[of, pl.ds(where * half, half), :].reshape(LANES, LANES).T
        gated_ref[:, lanes] = (gate_ref[:, lanes].astype(jnp.float32) * convolved).astype(jnp.bfloat16)
        gate_grad_ref[:, lanes] = (upstream_ref[:, lanes].astype(jnp.float32) * convolved).astype(jnp.bfloat16)
        input_grad = arrived_ref[of, pl.ds(width + where * half, half), :].reshape(LANES, LANES).T
        input_grad_ref[:, lanes] = input_grad.astype(jnp.bfloat16)
    for tile in range(per_half):
        lanes = pl.ds(tile * LANES, LANES)
        filter_grad_ref[:, lanes] = arrived_ref[pl.ds(tile * group, group), pl.ds(2 * width, half), :].reshape(LANES, LANES).T


def pack_plain(signal, gate, taps, upstream, seqs, half):
    own = lax.axis_index("dp")
    by_owner = lambda value, parts: value.T.reshape(parts, -1, half, value.shape[0]).transpose(1, 0, 2, 3).reshape(-1, parts * half, value.shape[0])
    taps = lax.dynamic_slice_in_dim(taps, own * (taps.shape[1] // seqs), taps.shape[1] // seqs, 1)
    carried = upstream.astype(jnp.float32) * gate.astype(jnp.float32)
    return jnp.concatenate([by_owner(signal.astype(jnp.float32), seqs), by_owner(carried, seqs), by_owner(taps, 1)], axis=1)


def core_plain(arrived, blocks, seqs, half, scale):
    width = seqs * half
    rows = arrived.shape[-1]
    mine = arrived.reshape(blocks, seqs, (2 * seqs + 1) * half, rows)
    taps = mine[:, :, 2 * width :].reshape(blocks, 1, width, rows)
    columns = jnp.concatenate([mine[:, :, :width], mine[:, :, width : 2 * width], taps], axis=1)
    angle = 2.0 * np.pi * (np.outer(np.arange(blocks + 1), np.arange(blocks)) % (2 * blocks)) / (2 * blocks)
    cos_block, sin_block = jnp.asarray(np.cos(angle), jnp.float32), jnp.asarray(np.sin(angle), jnp.float32)
    cosine, sine = (jnp.asarray(table, jnp.float32)[:, None, None] for table in residue_table(blocks + 1, rows))
    table = jnp.asarray(block_table(rows), jnp.float32)
    einsum = functools.partial(jnp.einsum, precision=HIGHEST)
    real, imag = einsum("kp,pgct->kgct", cos_block, columns), -einsum("kp,pgct->kgct", sin_block, columns)
    real, imag = real * cosine + imag * sine, imag * cosine - real * sine
    spec = einsum("kgct,tf->kgcf", jnp.concatenate([real, imag], axis=-1), table)
    spec = lax.complex(spec[..., :rows], spec[..., rows:])
    x, carried, taps = spec[:, :seqs], spec[:, seqs : 2 * seqs], spec[:, 2 * seqs :]
    filt = jnp.sum(carried * jnp.conj(x), axis=1, keepdims=True) * scale
    spec = jnp.concatenate([x * taps, carried * jnp.conj(taps), filt], axis=1)
    back = einsum("kgct,tf->kgcf", jnp.concatenate([spec.real, -spec.imag], axis=-1), table)
    real, imag = back[..., :rows], -back[..., rows:]
    real, imag = real * cosine - imag * sine, imag * cosine + real * sine
    weight = np.full((blocks + 1, 1), 2.0)
    weight[0] = weight[-1] = 1.0
    weight = jnp.asarray(weight / (2 * blocks * rows), jnp.float32)
    out = einsum("kp,kgct->pgct", cos_block * weight, real) - einsum("kp,kgct->pgct", sin_block * weight, imag)
    filt = out[:, 2 * seqs :].reshape(blocks, seqs, half, rows)
    return jnp.concatenate([out[:, :seqs], out[:, seqs : 2 * seqs], filt], axis=2).reshape(arrived.shape)


def unpack_plain(arrived, gate, upstream, seqs, half):
    width = seqs * half
    whole = lambda value, parts: value.reshape(-1, parts, half, value.shape[-1]).transpose(1, 0, 2, 3).reshape(-1, value.shape[-1]).T
    convolved = whole(arrived[:, :width], seqs)
    return (
        (gate.astype(jnp.float32) * convolved).astype(jnp.bfloat16),
        (upstream.astype(jnp.float32) * convolved).astype(jnp.bfloat16),
        whole(arrived[:, width : 2 * width], seqs).astype(jnp.bfloat16),
        whole(arrived[:, 2 * width :], 1),
    )


def shards(hyena_input, gate_input, filter_taps, cotangent):
    signal, gate, upstream = hyena_input[0], gate_input[0], cotangent[0]
    rows, channels = signal.shape
    blocks, seqs = lax.axis_size("context"), lax.axis_size("dp")
    owners = blocks * seqs
    half = channels // owners // seqs
    scale = 1.0 / math.sqrt(seqs * blocks * rows)
    tiled = rows == LANES and half % 8 == 0 and LANES % half == 0 and channels // seqs % LANES == 0
    vmem = pl.BlockSpec(memory_space=pltpu.VMEM)
    if tiled:
        leaving = pl.pallas_call(
            functools.partial(pack_kernel, seqs, half),
            out_shape=jax.ShapeDtypeStruct((owners, (2 * seqs + 1) * half, rows), jnp.float32),
            in_specs=[vmem] * 4,
            out_specs=vmem,
            name="pack",
        )(signal, gate, filter_taps, upstream)
    else:
        leaving = pack_plain(signal, gate, filter_taps, upstream, seqs, half)
    arrived = lax.all_to_all(leaving, ("context", "dp"), 0, 0, tiled=True)
    leaving = (core if tiled else core_plain)(arrived, blocks, seqs, half, scale)
    arrived = lax.all_to_all(leaving, ("context", "dp"), 0, 0, tiled=True)
    if tiled:
        wide = jax.ShapeDtypeStruct((rows, channels), jnp.bfloat16)
        gated, gate_grad, input_grad, filter_grad = pl.pallas_call(
            functools.partial(unpack_kernel, seqs, half),
            out_shape=(wide, wide, wide, jax.ShapeDtypeStruct((rows, channels // seqs), jnp.float32)),
            in_specs=[vmem] * 3,
            out_specs=(vmem,) * 4,
            name="unpack",
        )(arrived, gate, upstream)
    else:
        gated, gate_grad, input_grad, filter_grad = unpack_plain(arrived, gate, upstream, seqs, half)
    return gated[None], gate_grad[None], input_grad[None], filter_grad


def solution(mesh):
    placed = P(("groups", "dp"), "context", None)
    return jax.shard_map(
        shards,
        mesh=mesh,
        in_specs=(placed, placed, P("context", "groups"), placed),
        out_specs=(placed, placed, placed, P("context", ("groups", "dp"))),
        check_vma=False,
    )
```

profile of v0, /device:TPU:0, one launch (start us, length us, event | category | flops | bytes accessed | tf_op | source)
XLA Modules:
  0.0 54.1 jit_solution(13272616035595801369)
XLA Ops:
  0.6 2.2 %pack.1 = f32[16,80,128]{2,1,0:T(8,128)} custom-call(bf16[128,512]{1,0:T(8,128)(2,1)} %bitcast.10, bf16[128,512]{1,0:T(8,128)(2,1)} %bitcast.6, f32[128,512]{1,0:T(8,128)} %taps_ref.1, bf16[128,512]{1,0:T(8,128)(2,1)} %bitcast.8), custom_call_target="tpu_custom_call" | custom-call | tf_op jit(solution)/shard_map/pack/pallas_call | solution.py:268
  2.8 0.0 copy-start
  2.8 0.0 copy-start.1
  2.8 0.0 copy-start.2
  2.8 0.0 copy-start.3
  2.8 25.8 %all_to_all.10.arrived_ref = f32[16,80,128]{2,1,0:T(8,128)S(1)} all-to-all(f32[16,80,128]{2,1,0:T(8,128)} %pack.1), channel_id=1, replica_groups=mesh['groups'=2,'context'=8,'dp'=2] {'context','dp'}, dimensions={0} | all-to-all | bytes 1310720 | tf_op jit(solution)/shard_map/all_to_all | solution.py:277
  28.6 0.0 copy-done
  28.6 0.0 copy-done.1
  28.6 0.0 copy-done.2
  28.6 0.0 copy-done.3
  28.6 1.9 %core.1 = f32[16,80,128]{2,1,0:T(8,128)S(1)} custom-call(f32[16,80,128]{2,1,0:T(8,128)S(1)} %all_to_all.10.arrived_ref, bf16[256,256]{1,0:T(8,128)(2,1)S(1)} %copy-done.1, bf16[256,256]{1,0:T(8,128)(2,1)S(1)} %copy-done, f32[9,128]{1,0:T(8,128)S(1)} %copy-done.3, f32[9,128]{1,0:T(8,128)S(1)} %copy-done.2), custom_call_target="tpu_custom_call" | custom-call | tf_op jit(solution)/shard_map/core/pallas_call | solution.py:162
  30.5 21.5 %all_to_all.11.arrived_ref = f32[16,80,128]{2,1,0:T(8,128)} all-to-all(f32[16,80,128]{2,1,0:T(8,128)S(1)} %core.1), channel_id=1, replica_groups=mesh['groups'=2,'context'=8,'dp'=2] {'context','dp'}, dimensions={0} | all-to-all | bytes 1310720 | tf_op jit(solution)/shard_map/all_to_all | solution.py:279
  52.0 2.1 %unpack.1 = (bf16[128,512]{1,0:T(8,128)(2,1)}, bf16[128,512]{1,0:T(8,128)(2,1)}, bf16[128,512]{1,0:T(8,128)(2,1)}, f32[128,256]{1,0:T(8,128)}) custom-call(f32[16,80,128]{2,1,0:T(8,128)} %all_to_all.11.arrived_ref, bf16[128,512]{1,0:T(8,128)(2,1)} %bitcast.7, bf16[128,512]{1,0:T(8,128)(2,1)} %bitcast.9), custom_call_target="tpu_custom_call" | custom-call | tf_op jit(solution)/shard_map/unpack/pallas_call | solution.py:282
Async XLA Ops:
  2.8 25.8 %copy-start = (bf16[256,256]{1,0:T(8,128)(2,1)S(1)}, bf16[256,256]{1,0:T(8,128)(2,1)}, u32[]{:S(2)}) copy-start(bf16[256,256]{1,0:T(8,128)(2,1)} %constant.9.clone.low_ref) | copy-start | bytes 393220
  2.8 25.8 %copy-start.1 = (bf16[256,256]{1,0:T(8,128)(2,1)S(1)}, bf16[256,256]{1,0:T(8,128)(2,1)}, u32[]{:S(2)}) copy-start(bf16[256,256]{1,0:T(8,128)(2,1)} %constant.8.clone.high_ref) | copy-start | bytes 393220
  2.8 25.8 %copy-start.2 = (f32[9,128]{1,0:T(8,128)S(1)}, f32[9,128]{1,0:T(8,128)}, u32[]{:S(2)}) copy-start(f32[9,128]{1,0:T(8,128)} %constant.11.clone.sin_ref) | copy-start | bytes 13828
  2.8 25.8 %copy-start.3 = (f32[9,128]{1,0:T(8,128)S(1)}, f32[9,128]{1,0:T(8,128)}, u32[]{:S(2)}) copy-start(f32[9,128]{1,0:T(8,128)} %constant.10.clone.cos_ref) | copy-start | bytes 13828
where the time goes:
time: 54.4 us; the launch traced here: 54.1 us
  blocking collectives  47.3 us (87%)
  Pallas kernels  6.18 us (11%)
  between operations  0.66 us (1%)
    all_to_all x2, blocking collectives, shards(): arrived = lax.all_to_all(leaving, ('context', 'dp'), 0, 0, tiled=True)  47.3 us
    pallas_call x1, Pallas kernels, shards(): pl.pallas_call(functools.partial(pack_kernel, seqs, half), out_shape=jax....  2.17 us
    pallas_call x1, Pallas kernels, shards(): pl.pallas_call(functools.partial(unpack_kernel, seqs, half), out_shape=(w...  2.13 us
    pallas_call x1, Pallas kernels, core(): pl.pallas_call(functools.partial(core_kernel, blocks, seqs, half, np.floa...  1.88 us

commit v1 on v0

v1 whole, which is shorter than its diff:
```python
import functools
import math

import jax
import jax.numpy as jnp
import numpy as np
from jax import lax
from jax.experimental import pallas as pl
from jax.experimental.pallas import tpu as pltpu
from jax.sharding import PartitionSpec as P

LANES = 128
LIMIT = 16 * 2**20
PARTS = 1
PACK_LIMIT = 56 * 2**20
ORDER = (4, 2, 5, 6, 3, 7, 1, 0)
HIGHEST = lax.Precision.HIGHEST


def block_table(rows):
    index = np.arange(rows)
    angle = 2.0 * np.pi * (np.outer(index, index) % rows) / rows
    cosine, sine = np.cos(angle), np.sin(angle)
    return np.block([[cosine, -sine], [sine, cosine]])


def residue_table(count, rows):
    angle = 2.0 * np.pi * np.outer(np.arange(count), np.arange(rows)) / (2 * (count - 1) * rows)
    return np.cos(angle), np.sin(angle)


def table_kernel(_, own_ref, table_ref, cos_ref, sin_ref, kept_ref):
    kept_ref[...] = own_ref[...]
    rows, count = cos_ref.shape[1], cos_ref.shape[0]
    grid = lambda height, axis: lax.broadcasted_iota(jnp.int32, (height, rows), axis)
    angle = (grid(rows, 0) * grid(rows, 1) % rows).astype(jnp.float32) * np.float32(2.0 * math.pi / rows)
    cosine, sine = jnp.cos(angle), jnp.sin(angle)
    for row, col, value in ((0, 0, cosine), (0, 1, -sine), (1, 0, sine), (1, 1, cosine)):
        high = value.astype(jnp.bfloat16)
        put = lambda part, piece: table_ref.__setitem__((pl.ds((2 * part + row) * rows, rows), pl.ds(col * rows, rows)), piece)
        put(0, high)
        put(1, high)
        put(2, (value - high.astype(jnp.float32)).astype(jnp.bfloat16))
    angle = (grid(count, 0) * grid(count, 1)).astype(jnp.float32) * np.float32(math.pi / ((count - 1) * rows))
    cos_ref[...] = jnp.cos(angle)
    sin_ref[...] = jnp.sin(angle)


def store_split(rows_ref, at, value):
    width = value.shape[1]
    high = value.astype(jnp.bfloat16)
    rows_ref[at, pl.ds(0, width)] = high
    rows_ref[at, pl.ds(width, width)] = (value - high.astype(jnp.float32)).astype(jnp.bfloat16)
    rows_ref[at, pl.ds(2 * width, width)] = high


def multiply(rows_ref, table_ref, out_ref, parts):
    size = rows_ref.shape[0] // parts
    for part in range(parts):
        at = pl.ds(part * size, size)
        out_ref[at, :] = jnp.dot(rows_ref[at, :], table_ref[...], preferred_element_type=jnp.float32)


def weighted(terms):
    total = None
    for weight, value in terms:
        if abs(weight) < 1e-12:
            continue
        if abs(weight - 1.0) < 1e-12:
            part = value
        elif abs(weight + 1.0) < 1e-12:
            total = -value if total is None else total - value
            continue
        else:
            part = value * np.float32(weight)
        total = part if total is None else total + part
    return total


def add(first, second):
    if first is None or second is None:
        return second if first is None else first
    return first + second


def sub(first, second):
    if second is None:
        return first
    return -second if first is None else first - second


def forward_sums(blocks, columns):
    turn = math.pi / blocks
    even, odd = range(0, blocks, 2), range(1, blocks, 2)
    sums = {}
    for k in range(blocks // 2 + 1):
        cos_even = weighted([(math.cos(turn * k * p), columns[p]) for p in even])
        cos_odd = weighted([(math.cos(turn * k * p), columns[p]) for p in odd])
        sin_even = weighted([(math.sin(turn * k * p), columns[p]) for p in even])
        sin_odd = weighted([(math.sin(turn * k * p), columns[p]) for p in odd])
        sums[k] = (add(cos_even, cos_odd), sub(sub(None, sin_even), sin_odd))
        if k != blocks - k:
            sums[blocks - k] = (sub(cos_even, cos_odd), sub(sin_even, sin_odd))
    return sums


def forward_rows(blocks, rows, load, cos_ref, sin_ref, rows_ref):
    for first in range(0, rows, 16):
        sums = forward_sums(blocks, [load(block, pl.ds(first, 16)) for block in range(blocks)])
        for k in range(blocks + 1):
            real, imag = sums[k]
            if k > 0:
                cosine, sine = cos_ref[pl.ds(k, 1), :], sin_ref[pl.ds(k, 1), :]
                if imag is None:
                    real, imag = real * cosine, -real * sine
                else:
                    real, imag = real * cosine + imag * sine, imag * cosine - real * sine
            imag = jnp.zeros_like(real) if imag is None else imag
            store_split(rows_ref, pl.ds(k * rows + first, 16), jnp.concatenate([real, imag], axis=1))


def times(first, second, conjugate):
    a, b, c, d = first[:, :LANES], first[:, LANES:], second[:, :LANES], second[:, LANES:]
    real, imag = (a * c + b * d, a * d - b * c) if conjugate else (a * c - b * d, -(a * d) - b * c)
    return jnp.concatenate([real, imag], axis=1)


def inverse_sums(blocks, rows, back_ref, cos_ref, sin_ref, put):
    turn = math.pi / blocks
    scale = 1.0 / (2 * blocks * LANES)
    for first in range(0, rows, 8):
        real, imag = [], [None] * (blocks + 1)
        for k in range(blocks + 1):
            at = pl.ds(k * rows + first, 8)
            weight = np.float32(scale if k in (0, blocks) else 2.0 * scale)
            one = back_ref[at, pl.ds(0, LANES)] * weight
            if k > 0:
                other = back_ref[at, pl.ds(LANES, LANES)] * weight
                cosine, sine = cos_ref[pl.ds(k, 1), :], sin_ref[pl.ds(k, 1), :]
                if k < blocks:
                    imag[k] = one * sine - other * cosine
                one = one * cosine + other * sine
            real.append(one)
        for block in range(blocks // 2 + 1):
            cos_even = weighted([(math.cos(turn * k * block), real[k]) for k in range(0, blocks + 1, 2)])
            cos_odd = weighted([(math.cos(turn * k * block), real[k]) for k in range(1, blocks, 2)])
            sin_even = weighted([(math.sin(turn * k * block), imag[k]) for k in range(2, blocks, 2)])
            sin_odd = weighted([(math.sin(turn * k * block), imag[k]) for k in range(1, blocks, 2)])
            put(block, first, sub(sub(add(cos_even, cos_odd), sin_even), sin_odd))
            if block not in (0, blocks - block):
                put(blocks - block, first, sub(add(sub(cos_even, cos_odd), sin_even), sin_odd))


def analyse_kernel(order, half, scale, *refs):
    blocks, size = len(order), 5 * half
    block_refs, (table_ref, cos_ref, sin_ref, spec_ref, keep_ref, swap_ref, held_ref, in_ref, out_ref, back_ref) = refs[:blocks], refs[blocks:]
    me = lax.axis_index("context")
    for step, block_ref in zip(order, block_refs):
        held_ref[me ^ step] = block_ref[...]
    for block in range(blocks):
        swap_ref[0, block] = held_ref[block, pl.ds(4 * half, half), :]
    forward_rows(blocks, size, lambda block, at: held_ref[block, at, :], cos_ref, sin_ref, in_ref)
    multiply(in_ref, table_ref, spec_ref, PARTS)
    for k in range(blocks + 1):
        for first in range(0, 2 * half, 16):
            at = lambda part: pl.ds(k * size + 2 * half * part + first, 16)
            store_split(out_ref, pl.ds(k * 2 * half + first, 16), times(spec_ref[at(1), :], spec_ref[at(0), :], True) * scale)
    multiply(out_ref, table_ref, back_ref, PARTS)

    def put(block, first, value):
        if first < half:
            keep_ref[block, pl.ds(first, 8), :] = value
        else:
            swap_ref[1, block, pl.ds(first - half, 8), :] = value

    inverse_sums(blocks, 2 * half, back_ref, cos_ref, sin_ref, put)


def combine_kernel(order, half, spec_ref, keep_ref, swapped_ref, table_ref, cos_ref, sin_ref, *refs):
    blocks, size = len(order), 5 * half
    block_refs, (held_ref, in_ref, taps_ref, out_ref, back_ref) = refs[:blocks], refs[blocks:]
    forward_rows(blocks, half, lambda block, at: swapped_ref[0, block, at, :], cos_ref, sin_ref, in_ref)
    multiply(in_ref, table_ref, taps_ref, 1)
    for k in range(blocks + 1):
        for first in range(0, 2 * half, 16):
            taps = spec_ref[pl.ds(k * size + 4 * half + first, 16), :] if first < half else taps_ref[pl.ds(k * half + first - half, 16), :]
            for part in range(2):
                spec = spec_ref[pl.ds(k * size + 2 * half * part + first, 16), :]
                store_split(out_ref, pl.ds(k * 4 * half + 2 * half * part + first, 16), times(spec, taps, part == 1))
    multiply(out_ref, table_ref, back_ref, PARTS)

    def put(block, first, value):
        held_ref[block, pl.ds(first, 8), :] = value

    inverse_sums(blocks, 4 * half, back_ref, cos_ref, sin_ref, put)
    for block in range(blocks):
        held_ref[block, pl.ds(4 * half, half), :] = keep_ref[block] + swapped_ref[1, block]
    me = lax.axis_index("context")
    for step, block_ref in zip(order, block_refs):
        block_ref[...] = held_ref[me ^ step]


def lanes_of(tile, per_half):
    start = (lax.axis_index("dp") ^ (tile // per_half)) * (per_half * LANES) + tile % per_half * LANES
    return pl.ds(pl.multiple_of(start, LANES), LANES)


def pack_kernel(order, half, *refs):
    blocks = len(order)
    signal_hbm, gate_hbm, taps_hbm, upstream_hbm = refs[:4]
    block_refs, (held_ref, signal_ref, gate_ref, taps_ref, upstream_ref, arrived) = refs[4 : 4 + blocks], refs[4 + blocks :]
    group = LANES // half
    per_half = signal_ref.shape[1] // 2 // LANES
    own = pl.ds(pl.multiple_of(lax.axis_index("dp") * (per_half * LANES), LANES), per_half * LANES)
    pairs = [(upstream_hbm, upstream_ref), (gate_hbm, gate_ref), (signal_hbm, signal_ref), (taps_hbm.at[:, own], taps_ref)]
    copies = [pltpu.make_async_copy(*pair, arrived.at[i]) for i, pair in enumerate(pairs)]
    for copy in copies:
        copy.start()

    def store(tile, row, value):
        held_ref[pl.ds(tile % per_half * group, group), pl.ds(row, half), :] = value.T.reshape(group, half, LANES)

    for copy in copies[:2]:
        copy.wait()
    for tile in range(2 * per_half):
        lanes = lanes_of(tile, per_half)
        carried = upstream_ref[:, lanes].astype(jnp.float32) * gate_ref[:, lanes].astype(jnp.float32)
        store(tile, (2 + tile // per_half) * half, carried)
    copies[2].wait()
    for tile in range(2 * per_half):
        store(tile, tile // per_half * half, signal_ref[:, lanes_of(tile, per_half)].astype(jnp.float32))
    copies[3].wait()
    for tile in range(per_half):
        store(tile, 4 * half, taps_ref[:, pl.ds(tile * LANES, LANES)])
    me = lax.axis_index("context")
    for step, block_ref in zip(order, block_refs):
        block_ref[...] = held_ref[me ^ step]


def unpack_kernel(order, half, *refs):
    blocks = len(order)
    block_refs, (gate_ref, upstream_ref, gated_ref, gate_grad_ref, input_grad_ref, filter_grad_ref, held_ref) = refs[:blocks], refs[blocks:]
    me = lax.axis_index("context")
    for step, block_ref in zip(order, block_refs):
        held_ref[me ^ step] = block_ref[...]
    group = LANES // half
    per_half = gate_ref.shape[1] // 2 // LANES
    for tile in range(2 * per_half):
        lanes = lanes_of(tile, per_half)
        of, row = pl.ds(tile % per_half * group, group), tile // per_half * half
        convolved = held_ref[of, pl.ds(row, half), :].reshape(LANES, LANES).T
        gated_ref[:, lanes] = (gate_ref[:, lanes].astype(jnp.float32) * convolved).astype(jnp.bfloat16)
        gate_grad_ref[:, lanes] = (upstream_ref[:, lanes].astype(jnp.float32) * convolved).astype(jnp.bfloat16)
        input_grad_ref[:, lanes] = held_ref[of, pl.ds(2 * half + row, half), :].reshape(LANES, LANES).T.astype(jnp.bfloat16)
        if tile < per_half:
            filter_grad_ref[:, pl.ds(tile * LANES, LANES)] = held_ref[of, pl.ds(4 * half, half), :].reshape(LANES, LANES).T


def exchange(parts, order):
    devices = lax.axis_size("context")
    send = lambda part, step: lax.ppermute(part, "context", [(place, place ^ step) for place in range(devices)])
    return [part if step == 0 else send(part, step) for part, step in zip(parts, order)]


def tiled_shards(signal, gate, taps, upstream, blocks, half, scale):
    rows, channels = signal.shape
    steps = [step for step in ORDER if step < blocks]
    order = steps + [step for step in range(blocks) if step not in steps]
    f32 = lambda *shape: jax.ShapeDtypeStruct(shape, jnp.float32)
    scratch = lambda *shape: pltpu.VMEM(shape, jnp.float32)
    split = lambda count: pltpu.VMEM(((blocks + 1) * count, 6 * rows), jnp.bfloat16)

    def call(kernel, name, inputs, outputs, scratches, space=pltpu.VMEM, limit=LIMIT):
        return pl.pallas_call(
            kernel,
            out_shape=outputs,
            in_specs=[pl.BlockSpec(memory_space=space)] * len(inputs),
            out_specs=[pl.BlockSpec(memory_space=pltpu.VMEM)] * len(outputs),
            scratch_shapes=scratches,
            compiler_params=pltpu.CompilerParams(vmem_limit_bytes=limit),
            name=name,
        )(*inputs)

    size = 5 * half
    held = scratch(blocks, size, rows)
    narrow = lambda *shape: pltpu.VMEM(shape, jnp.bfloat16)
    leaving = call(
        functools.partial(pack_kernel, order, half),
        "pack",
        [signal, gate, taps, upstream],
        [f32(size, rows)] * blocks,
        [held, narrow(rows, channels), narrow(rows, channels), scratch(rows, channels // 2), narrow(rows, channels), pltpu.SemaphoreType.DMA((4,))],
        pltpu.HBM,
        PACK_LIMIT,
    )
    arrived = exchange(leaving, order)
    *tables, arrived[-1] = call(
        table_kernel,
        "tables",
        [arrived[0], arrived[-1]],
        [jax.ShapeDtypeStruct((6 * rows, 2 * rows), jnp.bfloat16), f32(blocks + 1, rows), f32(blocks + 1, rows), f32(size, rows)],
        [],
    )
    spec, keep, swap = call(
        functools.partial(analyse_kernel, order, half, np.float32(scale)),
        "analyse",
        [*arrived, *tables],
        [f32((blocks + 1) * size, 2 * rows), f32(blocks, half, rows), f32(2, blocks, half, rows)],
        [held, split(size), split(2 * half), scratch((blocks + 1) * 2 * half, 2 * rows)],
    )
    swapped = lax.ppermute(swap, "dp", [(0, 1), (1, 0)])
    leaving = call(
        functools.partial(combine_kernel, order, half),
        "combine",
        [spec, keep, swapped, *tables],
        [f32(size, rows)] * blocks,
        [held, split(half), scratch((blocks + 1) * half, 2 * rows), split(4 * half), scratch((blocks + 1) * 4 * half, 2 * rows)],
    )
    arrived = exchange(leaving, order)
    wide = jax.ShapeDtypeStruct((rows, channels), jnp.bfloat16)
    return call(
        functools.partial(unpack_kernel, order, half),
        "unpack",
        [*arrived, gate, upstream],
        [wide, wide, wide, f32(rows, channels // 2)],
        [held],
    )


def pack_plain(signal, gate, taps, upstream, seqs, half):
    own = lax.axis_index("dp")
    by_owner = lambda value, parts: value.T.reshape(parts, -1, half, value.shape[0]).transpose(1, 0, 2, 3).reshape(-1, parts * half, value.shape[0])
    taps = lax.dynamic_slice_in_dim(taps, own * (taps.shape[1] // seqs), taps.shape[1] // seqs, 1)
    carried = upstream.astype(jnp.float32) * gate.astype(jnp.float32)
    return jnp.concatenate([by_owner(signal.astype(jnp.float32), seqs), by_owner(carried, seqs), by_owner(taps, 1)], axis=1)


def core_plain(arrived, blocks, seqs, half, scale):
    width = seqs * half
    rows = arrived.shape[-1]
    mine = arrived.reshape(blocks, seqs, (2 * seqs + 1) * half, rows)
    taps = mine[:, :, 2 * width :].reshape(blocks, 1, width, rows)
    columns = jnp.concatenate([mine[:, :, :width], mine[:, :, width : 2 * width], taps], axis=1)
    angle = 2.0 * np.pi * (np.outer(np.arange(blocks + 1), np.arange(blocks)) % (2 * blocks)) / (2 * blocks)
    cos_block, sin_block = jnp.asarray(np.cos(angle), jnp.float32), jnp.asarray(np.sin(angle), jnp.float32)
    cosine, sine = (jnp.asarray(table, jnp.float32)[:, None, None] for table in residue_table(blocks + 1, rows))
    table = jnp.asarray(block_table(rows), jnp.float32)
    einsum = functools.partial(jnp.einsum, precision=HIGHEST)
    real, imag = einsum("kp,pgct->kgct", cos_block, columns), -einsum("kp,pgct->kgct", sin_block, columns)
    real, imag = real * cosine + imag * sine, imag * cosine - real * sine
    spec = einsum("kgct,tf->kgcf", jnp.concatenate([real, imag], axis=-1), table)
    spec = lax.complex(spec[..., :rows], spec[..., rows:])
    x, carried, taps = spec[:, :seqs], spec[:, seqs : 2 * seqs], spec[:, 2 * seqs :]
    filt = jnp.sum(carried * jnp.conj(x), axis=1, keepdims=True) * scale
    spec = jnp.concatenate([x * taps, carried * jnp.conj(taps), filt], axis=1)
    back = einsum("kgct,tf->kgcf", jnp.concatenate([spec.real, -spec.imag], axis=-1), table)
    real, imag = back[..., :rows], -back[..., rows:]
    real, imag = real * cosine - imag * sine, imag * cosine + real * sine
    weight = np.full((blocks + 1, 1), 2.0)
    weight[0] = weight[-1] = 1.0
    weight = jnp.asarray(weight / (2 * blocks * rows), jnp.float32)
    out = einsum("kp,kgct->pgct", cos_block * weight, real) - einsum("kp,kgct->pgct", sin_block * weight, imag)
    filt = out[:, 2 * seqs :].reshape(blocks, seqs, half, rows)
    return jnp.concatenate([out[:, :seqs], out[:, seqs : 2 * seqs], filt], axis=2).reshape(arrived.shape)


def unpack_plain(arrived, gate, upstream, seqs, half):
    width = seqs * half
    whole = lambda value, parts: value.reshape(-1, parts, half, value.shape[-1]).transpose(1, 0, 2, 3).reshape(-1, value.shape[-1]).T
    convolved = whole(arrived[:, :width], seqs)
    return (
        (gate.astype(jnp.float32) * convolved).astype(jnp.bfloat16),
        (upstream.astype(jnp.float32) * convolved).astype(jnp.bfloat16),
        whole(arrived[:, width : 2 * width], seqs).astype(jnp.bfloat16),
        whole(arrived[:, 2 * width :], 1),
    )


def shards(hyena_input, gate_input, filter_taps, cotangent):
    signal, gate, upstream = hyena_input[0], gate_input[0], cotangent[0]
    rows, channels = signal.shape
    blocks, seqs = lax.axis_size("context"), lax.axis_size("dp")
    owners = blocks * seqs
    half = channels // owners // seqs
    scale = 1.0 / math.sqrt(seqs * blocks * rows)
    if seqs == 2 and blocks in (2, 4, 8) and rows == LANES and channels % (2 * LANES) == 0 and channels // blocks in (16, 32, 64, 128, 256):
        outputs = tiled_shards(signal, gate, filter_taps, upstream, blocks, channels // blocks // 2, scale)
    else:
        leaving = pack_plain(signal, gate, filter_taps, upstream, seqs, half)
        arrived = lax.all_to_all(leaving, ("context", "dp"), 0, 0, tiled=True)
        leaving = core_plain(arrived, blocks, seqs, half, scale)
        arrived = lax.all_to_all(leaving, ("context", "dp"), 0, 0, tiled=True)
        outputs = unpack_plain(arrived, gate, upstream, seqs, half)
    gated, gate_grad, input_grad, filter_grad = outputs
    return gated[None], gate_grad[None], input_grad[None], filter_grad


def solution(mesh):
    placed = P(("groups", "dp"), "context", None)
    return jax.shard_map(
        shards,
        mesh=mesh,
        in_specs=(placed, placed, P("context", "groups"), placed),
        out_specs=(placed, placed, placed, P("context", ("groups", "dp"))),
        check_vma=False,
    )
```

time: 54.4 us -> 44.8 us (0.82)
  blocking collectives: 47.3 us -> 0 us
  starting transfers between devices: 0 us -> 24.2 us
  waiting for transfers between devices: 0 us -> 12.4 us
  local copies, waits for them, and re-layouts: 0.01 us -> 0.89 us
    all_to_all x2 -> x0, blocking collectives: 47.3 us -> none  [shards(): arrived = lax.all_to_all(leaving, ('context', 'dp'), 0, 0, tiled=True)]
    ppermute x0 -> x15, starting transfers between devices: none -> 24.2 us  [the longest x14 24.2 us: exchange(): lax.ppermute(part, 'context', [(place, place ^ step) for place in range(d...]
    ppermute x0 -> x15, waiting for transfers between devices: none -> 12.4 us  [the longest x14 10.9 us: exchange(): lax.ppermute(part, 'context', [(place, place ^ step) for place in range(d...]
    unnamed x8 -> x6, local copies, waits for them, and re-layouts: 0.01 us -> 0.89 us
    pallas_call x3 -> x5, Pallas kernels: 6.18 us -> 6.42 us  [call(): pl.pallas_call(kernel, out_shape=outputs, in_specs=[pl.BlockSpec(memory_s...]
  transfers between devices with their start and end apart: 0 -> 15, of which waited for: 0 -> 9; matrix products, arithmetic and copies ran while one was open for 0% -> 0% of each run, Pallas kernels for 0% -> 1%
where the time goes in v1:
time: 44.8 us; the launch traced here: 44.6 us
  starting transfers between devices  24.2 us (54%)
  waiting for transfers between devices  12.4 us (28%)
  Pallas kernels  6.42 us (14%)
  local copies, waits for them, and re-layouts  0.89 us (2%)
  between operations  0.68 us (2%)
    ppermute x14, starting transfers between devices, exchange(): lax.ppermute(part, 'context', [(place, place ^ step) for place in range(d...  24.2 us
    ppermute x14, waiting for transfers between devices, exchange(): lax.ppermute(part, 'context', [(place, place ^ step) for place in range(d...  10.9 us
    pallas_call x5, Pallas kernels, call(): pl.pallas_call(kernel, out_shape=outputs, in_specs=[pl.BlockSpec(memory_s...  6.42 us
    ppermute x1, waiting for transfers between devices, tiled_shards(): swapped = lax.ppermute(swap, 'dp', [(0, 1), (1, 0)])  1.52 us
  transfers between devices with their start and end apart: 15, of which 9 were waited for; matrix products, arithmetic and copies ran while one was open for 0% of the time, Pallas kernels for 1%

profile of v1, /device:TPU:0, one launch (start us, length us, event | category | flops | bytes accessed | tf_op | source)
XLA Modules:
  0.0 44.6 jit_solution(11456452271923276986)
XLA Ops:
  0.6 2.2 %pack.1 = (f32[160,128]{1,0:T(8,128)}, f32[160,128]{1,0:T(8,128)}, f32[160,128]{1,0:T(8,128)}, f32[160,128]{1,0:T(8,128)}, f32[160,128]{1,0:T(8,128)}, /*index=5...) custom-call(bf16[128,512]{1,0:T(8,128)(2,1)} %bitcast.10, bf16[128,512]{1,0:T(8,128)(2,1)} %bitcast.6, ...), custom_call_target="tpu_custom_call" | custom-call | tf_op jit(solution)/shard_map/pack/pallas_call | solution.py:274
  2.8 4.1 %collective-permute-start = (f32[160,128]{1,0:T(8,128)}, f32[160,128]{1,0:T(8,128)S(1)}, u32[]{:S(2)}, u32[]{:S(2)}) collective-permute-start(f32[160,128]{1,0:T(8,128)} %get-tuple-element.31), channel_id=1, source_target_pairs={{0,8},{2,10},{4,12},{6,14},{8,0},{10,2},{12,4},{14,6},{1,9},{3,11}... | collective-permute-start | bytes 245768 | tf_op jit(solution)/shard_map/ppermute | solution.py:261
  6.9 1.6 %collective-permute-start.1 = (f32[160,128]{1,0:T(8,128)}, f32[160,128]{1,0:T(8,128)S(1)}, u32[]{:S(2)}, u32[]{:S(2)}) collective-permute-start(f32[160,128]{1,0:T(8,128)} %get-tuple-element.32), channel_id=1, source_target_pairs={{0,4},{2,6},{4,0},{6,2},{8,12},{10,14},{12,8},{14,10},{1,5},{3,7},... | collective-permute-start | bytes 245768 | tf_op jit(solution)/shard_map/ppermute | solution.py:261
  8.5 1.3 %collective-permute-start.2 = (f32[160,128]{1,0:T(8,128)}, f32[160,128]{1,0:T(8,128)S(1)}, u32[]{:S(2)}, u32[]{:S(2)}) collective-permute-start(f32[160,128]{1,0:T(8,128)} %get-tuple-element.33), channel_id=1, source_target_pairs={{0,10},{2,8},{4,14},{6,12},{8,2},{10,0},{12,6},{14,4},{1,11},{3,9}... | collective-permute-start | bytes 245768 | tf_op jit(solution)/shard_map/ppermute | solution.py:261
  9.8 2.5 %collective-permute-start.3 = (f32[160,128]{1,0:T(8,128)}, f32[160,128]{1,0:T(8,128)S(1)}, u32[]{:S(2)}, u32[]{:S(2)}) collective-permute-start(f32[160,128]{1,0:T(8,128)} %get-tuple-element.34), channel_id=1, source_target_pairs={{0,12},{2,14},{4,8},{6,10},{8,4},{10,6},{12,0},{14,2},{1,13},{3,15... | collective-permute-start | bytes 245768 | tf_op jit(solution)/shard_map/ppermute | solution.py:261
  12.3 0.6 %collective-permute-start.4 = (f32[160,128]{1,0:T(8,128)}, f32[160,128]{1,0:T(8,128)S(1)}, u32[]{:S(2)}, u32[]{:S(2)}) collective-permute-start(f32[160,128]{1,0:T(8,128)} %get-tuple-element.35), channel_id=1, source_target_pairs={{0,6},{2,4},{4,2},{6,0},{8,14},{10,12},{12,10},{14,8},{1,7},{3,5},... | collective-permute-start | bytes 245768 | tf_op jit(solution)/shard_map/ppermute | solution.py:261
  12.9 0.0 collective-permute-done._.refs_0_
  12.9 3.9 %collective-permute-start.5 = (f32[160,128]{1,0:T(8,128)}, f32[160,128]{1,0:T(8,128)S(1)}, u32[]{:S(2)}, u32[]{:S(2)}) collective-permute-start(f32[160,128]{1,0:T(8,128)} %get-tuple-element.36), channel_id=1, source_target_pairs={{0,14},{2,12},{4,10},{6,8},{8,6},{10,4},{12,2},{14,0},{1,15},{3,13... | collective-permute-start | bytes 245768 | tf_op jit(solution)/shard_map/ppermute | solution.py:261
  16.8 0.0 collective-permute-done.1.refs_1_
  16.8 0.5 %collective-permute-start.6 = (f32[160,128]{1,0:T(8,128)}, f32[160,128]{1,0:T(8,128)S(1)}, u32[]{:S(2)}, u32[]{:S(2)}) collective-permute-start(f32[160,128]{1,0:T(8,128)} %get-tuple-element.37), channel_id=1, source_target_pairs={{0,2},{2,0},{4,6},{6,4},{8,10},{10,8},{12,14},{14,12},{1,3},{3,1},... | collective-permute-start | bytes 245768 | tf_op jit(solution)/shard_map/ppermute | solution.py:261
  17.3 0.0 copy-start.2
  17.3 0.9 %copy-done.2 = f32[160,128]{1,0:T(8,128)S(1)} copy-done((f32[160,128]{1,0:T(8,128)S(1)}, f32[160,128]{1,0:T(8,128)}, u32[]{:S(2)}) %copy-start.2) | copy-done | bytes 81944
  18.2 0.3 tables.1
  18.5 0.9 %collective-permute-done.2.refs_2_ = f32[160,128]{1,0:T(8,128)S(1)} collective-permute-done((f32[160,128]{1,0:T(8,128)}, f32[160,128]{1,0:T(8,128)S(1)}, u32[]{:S(2)}, u32[]{:S(2)}) %collective-permute-start.2) | collective-permute-done | bytes 81952 | tf_op jit(solution)/shard_map/ppermute | solution.py:261
  19.5 0.0 collective-permute-done.3.refs_3_
  19.5 1.2 %collective-permute-done.4.refs_4_ = f32[160,128]{1,0:T(8,128)S(1)} collective-permute-done((f32[160,128]{1,0:T(8,128)}, f32[160,128]{1,0:T(8,128)S(1)}, u32[]{:S(2)}, u32[]{:S(2)}) %collective-permute-start.4) | collective-permute-done | bytes 81952 | tf_op jit(solution)/shard_map/ppermute | solution.py:261
  20.7 0.0 collective-permute-done.5.refs_5_
  20.7 1.6 %collective-permute-done.6.refs_6_ = f32[160,128]{1,0:T(8,128)S(1)} collective-permute-done((f32[160,128]{1,0:T(8,128)}, f32[160,128]{1,0:T(8,128)S(1)}, u32[]{:S(2)}, u32[]{:S(2)}) %collective-permute-start.6) | collective-permute-done | bytes 81952 | tf_op jit(solution)/shard_map/ppermute | solution.py:261
  22.4 0.0 copy-start
  22.4 0.0 copy-start.1
  22.4 1.6 %analyse.1 = (f32[1440,256]{1,0:T(8,128)S(1)}, f32[8,32,128]{2,1,0:T(8,128)S(1)}, f32[2,8,32,128]{3,2,1,0:T(8,128)S(1)}) custom-call(f32[160,128]{1,0:T(8,128)S(1)} %collective-permute-done._.refs_0_, f32[160,128]{1,0:T(8,128)S(1)} %collective-permute-done.1.refs_1_, f32[160,128]{1,0:T(8,128)S(1)} %collective-permute-done.2.refs_2_, ...), custom_call_target="tpu_custom_call" | custom-call | tf_op jit(solution)/shard_map/analyse/pallas_call | solution.py:274
  24.0 0.1 collective-permute-start.7
  24.1 1.5 %collective-permute-done.7.swapped_ref = f32[2,8,32,128]{3,2,1,0:T(8,128)S(1)} collective-permute-done((f32[2,8,32,128]{3,2,1,0:T(8,128)S(1)}, f32[2,8,32,128]{3,2,1,0:T(8,128)S(1)}, u32[]{:S(2)}, u32[]{:S(2)}) %collective-permute-start.7) | collective-permute-done | bytes 262176 | tf_op jit(solution)/shard_map/ppermute | solution.py:311
  25.6 1.3 %combine.1 = (f32[160,128]{1,0:T(8,128)S(1)}, f32[160,128]{1,0:T(8,128)S(1)}, f32[160,128]{1,0:T(8,128)S(1)}, f32[160,128]{1,0:T(8,128)S(1)}, f32[160,128]{1,0:T...) custom-call(f32[1440,256]{1,0:T(8,128)S(1)} %get-tuple-element.43.spec_ref, ...), custom_call_target="tpu_custom_call" | custom-call | tf_op jit(solution)/shard_map/combine/pallas_call | solution.py:274
  26.9 3.2 %collective-permute-start.8 = (f32[160,128]{1,0:T(8,128)S(1)}, f32[160,128]{1,0:T(8,128)S(1)}, u32[]{:S(2)}, u32[]{:S(2)}) collective-permute-start(f32[160,128]{1,0:T(8,128)S(1)} %get-tuple-element.46), channel_id=1, source_target_pairs={{0,8},{2,10},{4,12},{6,14},{8,0},{10,2},{12,4},{14,6},{1,9},{3,11}... | collective-permute-start | bytes 245768 | tf_op jit(solution)/shard_map/ppermute | solution.py:261
  30.0 0.0 collective-permute-start.9
  30.0 1.9 %collective-permute-start.10 = (f32[160,128]{1,0:T(8,128)S(1)}, f32[160,128]{1,0:T(8,128)S(1)}, u32[]{:S(2)}, u32[]{:S(2)}) collective-permute-start(f32[160,128]{1,0:T(8,128)S(1)} %get-tuple-element.48), channel_id=1, source_target_pairs={{0,10},{2,8},{4,14},{6,12},{8,2},{10,0},{12,6},{14,4},{1,11},{3,9}... | collective-permute-start | bytes 245768 | tf_op jit(solution)/shard_map/ppermute | solution.py:261
  31.9 2.5 %collective-permute-start.11 = (f32[160,128]{1,0:T(8,128)S(1)}, f32[160,128]{1,0:T(8,128)S(1)}, u32[]{:S(2)}, u32[]{:S(2)}) collective-permute-start(f32[160,128]{1,0:T(8,128)S(1)} %get-tuple-element.49), channel_id=1, source_target_pairs={{0,12},{2,14},{4,8},{6,10},{8,4},{10,6},{12,0},{14,2},{1,13},{3,15... | collective-permute-start | bytes 245768 | tf_op jit(solution)/shard_map/ppermute | solution.py:261
  34.4 0.1 collective-permute-start.12
  34.4 0.6 %collective-permute-done.8.refs_0_ = f32[160,128]{1,0:T(8,128)S(1)} collective-permute-done((f32[160,128]{1,0:T(8,128)S(1)}, f32[160,128]{1,0:T(8,128)S(1)}, u32[]{:S(2)}, u32[]{:S(2)}) %collective-permute-start.8) | collective-permute-done | bytes 81952 | tf_op jit(solution)/shard_map/ppermute | solution.py:261
  35.0 1.3 %collective-permute-start.13 = (f32[160,128]{1,0:T(8,128)S(1)}, f32[160,128]{1,0:T(8,128)S(1)}, u32[]{:S(2)}, u32[]{:S(2)}) collective-permute-start(f32[160,128]{1,0:T(8,128)S(1)} %get-tuple-element.51), channel_id=1, source_target_pairs={{0,14},{2,12},{4,10},{6,8},{8,6},{10,4},{12,2},{14,0},{1,15},{3,13... | collective-permute-start | bytes 245768 | tf_op jit(solution)/shard_map/ppermute | solution.py:261
  36.3 0.3 collective-permute-done.9.refs_1_
  36.6 0.9 %collective-permute-start.14 = (f32[160,128]{1,0:T(8,128)S(1)}, f32[160,128]{1,0:T(8,128)S(1)}, u32[]{:S(2)}, u32[]{:S(2)}) collective-permute-start(f32[160,128]{1,0:T(8,128)S(1)} %get-tuple-element.52), channel_id=1, source_target_pairs={{0,2},{2,0},{4,6},{6,4},{8,10},{10,8},{12,14},{14,12},{1,3},{3,1},... | collective-permute-start | bytes 245768 | tf_op jit(solution)/shard_map/ppermute | solution.py:261
  37.4 4.2 %collective-permute-done.10.refs_2_ = f32[160,128]{1,0:T(8,128)S(1)} collective-permute-done((f32[160,128]{1,0:T(8,128)S(1)}, f32[160,128]{1,0:T(8,128)S(1)}, u32[]{:S(2)}, u32[]{:S(2)}) %collective-permute-start.10) | collective-permute-done | bytes 81952 | tf_op jit(solution)/shard_map/ppermute | solution.py:261
  41.6 0.0 collective-permute-done.11.refs_3_
  41.6 1.2 %collective-permute-done.12.refs_4_ = f32[160,128]{1,0:T(8,128)S(1)} collective-permute-done((f32[160,128]{1,0:T(8,128)S(1)}, f32[160,128]{1,0:T(8,128)S(1)}, u32[]{:S(2)}, u32[]{:S(2)}) %collective-permute-start.12) | collective-permute-done | bytes 81952 | tf_op jit(solution)/shard_map/ppermute | solution.py:261
  42.8 0.0 collective-permute-done.13.refs_5_
  42.8 0.8 %collective-permute-done.14.refs_6_ = f32[160,128]{1,0:T(8,128)S(1)} collective-permute-done((f32[160,128]{1,0:T(8,128)S(1)}, f32[160,128]{1,0:T(8,128)S(1)}, u32[]{:S(2)}, u32[]{:S(2)}) %collective-permute-start.14) | collective-permute-done | bytes 81952 | tf_op jit(solution)/shard_map/ppermute | solution.py:261
  43.6 0.0 copy-done
  43.6 0.0 copy-done.1
  43.6 1.0 %unpack.1 = (bf16[128,512]{1,0:T(8,128)(2,1)}, bf16[128,512]{1,0:T(8,128)(2,1)}, bf16[128,512]{1,0:T(8,128)(2,1)}, f32[128,256]{1,0:T(8,128)}) custom-call(f32[160,128]{1,0:T(8,128)S(1)} %collective-permute-done.8.refs_0_, f32[160,128]{1,0:T(8,128)S(1)} %collective-permute-done.9.refs_1_, f32[160,128]{1,0:T(8,128)S(1)} %collective-permute-done.10.refs_2_, ...), custom_call_target="tpu_custom_call" | custom-call | tf_op jit(solution)/shard_map/unpack/pallas_call | solution.py:274
Async XLA Ops:
  2.8 10.1 %collective-permute-start = (f32[160,128]{1,0:T(8,128)}, f32[160,128]{1,0:T(8,128)S(1)}, u32[]{:S(2)}, u32[]{:S(2)}) collective-permute-start(f32[160,128]{1,0:T(8,128)} %get-tuple-element.31), channel_id=1, source_target_pairs={{0,8},{2,10},{4,12},{6,14},{8,0},{10,2},{12,4},{14,6},{1,9},{3,11}... | collective-permute-start | bytes 245768 | tf_op jit(solution)/shard_map/ppermute | solution.py:261
  6.9 9.9 %collective-permute-start.1 = (f32[160,128]{1,0:T(8,128)}, f32[160,128]{1,0:T(8,128)S(1)}, u32[]{:S(2)}, u32[]{:S(2)}) collective-permute-start(f32[160,128]{1,0:T(8,128)} %get-tuple-element.32), channel_id=1, source_target_pairs={{0,4},{2,6},{4,0},{6,2},{8,12},{10,14},{12,8},{14,10},{1,5},{3,7},... | collective-permute-start | bytes 245768 | tf_op jit(solution)/shard_map/ppermute | solution.py:261
  8.5 11.0 %collective-permute-start.2 = (f32[160,128]{1,0:T(8,128)}, f32[160,128]{1,0:T(8,128)S(1)}, u32[]{:S(2)}, u32[]{:S(2)}) collective-permute-start(f32[160,128]{1,0:T(8,128)} %get-tuple-element.33), channel_id=1, source_target_pairs={{0,10},{2,8},{4,14},{6,12},{8,2},{10,0},{12,6},{14,4},{1,11},{3,9}... | collective-permute-start | bytes 245768 | tf_op jit(solution)/shard_map/ppermute | solution.py:261
  9.8 9.7 %collective-permute-start.3 = (f32[160,128]{1,0:T(8,128)}, f32[160,128]{1,0:T(8,128)S(1)}, u32[]{:S(2)}, u32[]{:S(2)}) collective-permute-start(f32[160,128]{1,0:T(8,128)} %get-tuple-element.34), channel_id=1, source_target_pairs={{0,12},{2,14},{4,8},{6,10},{8,4},{10,6},{12,0},{14,2},{1,13},{3,15... | collective-permute-start | bytes 245768 | tf_op jit(solution)/shard_map/ppermute | solution.py:261
  12.3 8.4 %collective-permute-start.4 = (f32[160,128]{1,0:T(8,128)}, f32[160,128]{1,0:T(8,128)S(1)}, u32[]{:S(2)}, u32[]{:S(2)}) collective-permute-start(f32[160,128]{1,0:T(8,128)} %get-tuple-element.35), channel_id=1, source_target_pairs={{0,6},{2,4},{4,2},{6,0},{8,14},{10,12},{12,10},{14,8},{1,7},{3,5},... | collective-permute-start | bytes 245768 | tf_op jit(solution)/shard_map/ppermute | solution.py:261
  12.9 7.8 %collective-permute-start.5 = (f32[160,128]{1,0:T(8,128)}, f32[160,128]{1,0:T(8,128)S(1)}, u32[]{:S(2)}, u32[]{:S(2)}) collective-permute-start(f32[160,128]{1,0:T(8,128)} %get-tuple-element.36), channel_id=1, source_target_pairs={{0,14},{2,12},{4,10},{6,8},{8,6},{10,4},{12,2},{14,0},{1,15},{3,13... | collective-permute-start | bytes 245768 | tf_op jit(solution)/shard_map/ppermute | solution.py:261
  16.8 5.6 %collective-permute-start.6 = (f32[160,128]{1,0:T(8,128)}, f32[160,128]{1,0:T(8,128)S(1)}, u32[]{:S(2)}, u32[]{:S(2)}) collective-permute-start(f32[160,128]{1,0:T(8,128)} %get-tuple-element.37), channel_id=1, source_target_pairs={{0,2},{2,0},{4,6},{6,4},{8,10},{10,8},{12,14},{14,12},{1,3},{3,1},... | collective-permute-start | bytes 245768 | tf_op jit(solution)/shard_map/ppermute | solution.py:261
  17.3 0.9 %copy-start.2 = (f32[160,128]{1,0:T(8,128)S(1)}, f32[160,128]{1,0:T(8,128)}, u32[]{:S(2)}) copy-start(f32[160,128]{1,0:T(8,128)} %get-tuple-element.38.own_ref) | copy-start | bytes 245764
  22.4 21.3 %copy-start = (bf16[1,128,512]{2,1,0:T(8,128)(2,1)S(1)}, bf16[1,128,512]{2,1,0:T(8,128)(2,1)}, u32[]{:S(2)}) copy-start(bf16[1,128,512]{2,1,0:T(8,128)(2,1)} %param.5) | copy-start | bytes 393220
  22.4 21.3 %copy-start.1 = (bf16[1,128,512]{2,1,0:T(8,128)(2,1)S(1)}, bf16[1,128,512]{2,1,0:T(8,128)(2,1)}, u32[]{:S(2)}) copy-start(bf16[1,128,512]{2,1,0:T(8,128)(2,1)} %param.7) | copy-start | bytes 393220
  24.0 1.6 %collective-permute-start.7 = (f32[2,8,32,128]{3,2,1,0:T(8,128)S(1)}, f32[2,8,32,128]{3,2,1,0:T(8,128)S(1)}, u32[]{:S(2)}, u32[]{:S(2)}) collective-permute-start(f32[2,8,32,128]{3,2,1,0:T(8,128)S(1)} %get-tuple-element.45), channel_id=1, source_target_pairs={{0,1},{1,0},{2,3},{3,2},{4,5},{5,4},{6,7},{7,6},{8,9},{9,8},{10,11... | collective-permute-start | bytes 786440 | tf_op jit(solution)/shard_map/ppermute | solution.py:311
  26.9 8.1 %collective-permute-start.8 = (f32[160,128]{1,0:T(8,128)S(1)}, f32[160,128]{1,0:T(8,128)S(1)}, u32[]{:S(2)}, u32[]{:S(2)}) collective-permute-start(f32[160,128]{1,0:T(8,128)S(1)} %get-tuple-element.46), channel_id=1, source_target_pairs={{0,8},{2,10},{4,12},{6,14},{8,0},{10,2},{12,4},{14,6},{1,9},{3,11}... | collective-permute-start | bytes 245768 | tf_op jit(solution)/shard_map/ppermute | solution.py:261
  30.0 6.5 %collective-permute-start.9 = (f32[160,128]{1,0:T(8,128)S(1)}, f32[160,128]{1,0:T(8,128)S(1)}, u32[]{:S(2)}, u32[]{:S(2)}) collective-permute-start(f32[160,128]{1,0:T(8,128)S(1)} %get-tuple-element.47), channel_id=1, source_target_pairs={{0,4},{2,6},{4,0},{6,2},{8,12},{10,14},{12,8},{14,10},{1,5},{3,7},... | collective-permute-start | bytes 245768 | tf_op jit(solution)/shard_map/ppermute | solution.py:261
  30.0 11.6 %collective-permute-start.10 = (f32[160,128]{1,0:T(8,128)S(1)}, f32[160,128]{1,0:T(8,128)S(1)}, u32[]{:S(2)}, u32[]{:S(2)}) collective-permute-start(f32[160,128]{1,0:T(8,128)S(1)} %get-tuple-element.48), channel_id=1, source_target_pairs={{0,10},{2,8},{4,14},{6,12},{8,2},{10,0},{12,6},{14,4},{1,11},{3,9}... | collective-permute-start | bytes 245768 | tf_op jit(solution)/shard_map/ppermute | solution.py:261
  31.9 9.7 %collective-permute-start.11 = (f32[160,128]{1,0:T(8,128)S(1)}, f32[160,128]{1,0:T(8,128)S(1)}, u32[]{:S(2)}, u32[]{:S(2)}) collective-permute-start(f32[160,128]{1,0:T(8,128)S(1)} %get-tuple-element.49), channel_id=1, source_target_pairs={{0,12},{2,14},{4,8},{6,10},{8,4},{10,6},{12,0},{14,2},{1,13},{3,15... | collective-permute-start | bytes 245768 | tf_op jit(solution)/shard_map/ppermute | solution.py:261
  34.4 8.5 %collective-permute-start.12 = (f32[160,128]{1,0:T(8,128)S(1)}, f32[160,128]{1,0:T(8,128)S(1)}, u32[]{:S(2)}, u32[]{:S(2)}) collective-permute-start(f32[160,128]{1,0:T(8,128)S(1)} %get-tuple-element.50), channel_id=1, source_target_pairs={{0,6},{2,4},{4,2},{6,0},{8,14},{10,12},{12,10},{14,8},{1,7},{3,5},... | collective-permute-start | bytes 245768 | tf_op jit(solution)/shard_map/ppermute | solution.py:261
  35.0 7.8 %collective-permute-start.13 = (f32[160,128]{1,0:T(8,128)S(1)}, f32[160,128]{1,0:T(8,128)S(1)}, u32[]{:S(2)}, u32[]{:S(2)}) collective-permute-start(f32[160,128]{1,0:T(8,128)S(1)} %get-tuple-element.51), channel_id=1, source_target_pairs={{0,14},{2,12},{4,10},{6,8},{8,6},{10,4},{12,2},{14,0},{1,15},{3,13... | collective-permute-start | bytes 245768 | tf_op jit(solution)/shard_map/ppermute | solution.py:261
  36.6 7.0 %collective-permute-start.14 = (f32[160,128]{1,0:T(8,128)S(1)}, f32[160,128]{1,0:T(8,128)S(1)}, u32[]{:S(2)}, u32[]{:S(2)}) collective-permute-start(f32[160,128]{1,0:T(8,128)S(1)} %get-tuple-element.52), channel_id=1, source_target_pairs={{0,2},{2,0},{4,6},{6,4},{8,10},{10,8},{12,14},{14,12},{1,3},{3,1},... | collective-permute-start | bytes 245768 | tf_op jit(solution)/shard_map/ppermute | solution.py:261

commit v2 on v1

--- a/solution.py
+++ b/solution.py
@@ -12,8 +12,9 @@
 LANES = 128
 LIMIT = 16 * 2**20
 PARTS = 1
-PACK_LIMIT = 56 * 2**20
-ORDER = (4, 2, 5, 6, 3, 7, 1, 0)
+PACK_LIMIT = 53 * 2**20 + 2**18
+ORDER = (4, 3, 5, 7, 2, 6, 1, 0)
+ORDER_BACK = (4, 3, 5, 7, 2, 6, 1, 0)
 HIGHEST = lax.Precision.HIGHEST
 
 
@@ -151,14 +152,18 @@
                 put(blocks - block, first, sub(add(sub(cos_even, cos_odd), sin_even), sin_odd))
 
 
+def gather_kernel(order, half, *refs):
+    me = lax.axis_index("context")
+    for step, block_ref in zip(order, refs[:-1]):
+        refs[-1][me ^ step] = block_ref[pl.ds(4 * half, half), :]
+
+
 def analyse_kernel(order, half, scale, *refs):
     blocks, size = len(order), 5 * half
     block_refs, (table_ref, cos_ref, sin_ref, spec_ref, keep_ref, swap_ref, held_ref, in_ref, out_ref, back_ref) = refs[:blocks], refs[blocks:]
     me = lax.axis_index("context")
     for step, block_ref in zip(order, block_refs):
         held_ref[me ^ step] = block_ref[...]
-    for block in range(blocks):
-        swap_ref[0, block] = held_ref[block, pl.ds(4 * half, half), :]
     forward_rows(blocks, size, lambda block, at: held_ref[block, at, :], cos_ref, sin_ref, in_ref)
     multiply(in_ref, table_ref, spec_ref, PARTS)
     for k in range(blocks + 1):
@@ -171,15 +176,14 @@
         if first < half:
             keep_ref[block, pl.ds(first, 8), :] = value
         else:
-            swap_ref[1, block, pl.ds(first - half, 8), :] = value
+            swap_ref[block, pl.ds(first - half, 8), :] = value
 
     inverse_sums(blocks, 2 * half, back_ref, cos_ref, sin_ref, put)
 
 
-def combine_kernel(order, half, spec_ref, keep_ref, swapped_ref, table_ref, cos_ref, sin_ref, *refs):
-    blocks, size = len(order), 5 * half
-    block_refs, (held_ref, in_ref, taps_ref, out_ref, back_ref) = refs[:blocks], refs[blocks:]
-    forward_rows(blocks, half, lambda block, at: swapped_ref[0, block, at, :], cos_ref, sin_ref, in_ref)
+def combine_kernel(blocks, half, spec_ref, swapped_ref, table_ref, cos_ref, sin_ref, held_ref, in_ref, taps_ref, out_ref, back_ref):
+    size = 5 * half
+    forward_rows(blocks, half, lambda block, at: swapped_ref[block, at, :], cos_ref, sin_ref, in_ref)
     multiply(in_ref, table_ref, taps_ref, 1)
     for k in range(blocks + 1):
         for first in range(0, 2 * half, 16):
@@ -193,11 +197,13 @@
         held_ref[block, pl.ds(first, 8), :] = value
 
     inverse_sums(blocks, 4 * half, back_ref, cos_ref, sin_ref, put)
-    for block in range(blocks):
-        held_ref[block, pl.ds(4 * half, half), :] = keep_ref[block] + swapped_ref[1, block]
+
+
+def finish_kernel(order, half, held_ref, keep_ref, swapped_ref, *block_refs):
     me = lax.axis_index("context")
     for step, block_ref in zip(order, block_refs):
-        block_ref[...] = held_ref[me ^ step]
+        block_ref[pl.ds(0, 4 * half), :] = held_ref[me ^ step]
+        block_ref[pl.ds(4 * half, half), :] = keep_ref[me ^ step] + swapped_ref[me ^ step]
 
 
 def lanes_of(tile, per_half):
@@ -264,8 +270,7 @@
 
 def tiled_shards(signal, gate, taps, upstream, blocks, half, scale):
     rows, channels = signal.shape
-    steps = [step for step in ORDER if step < blocks]
-    order = steps + [step for step in range(blocks) if step not in steps]
+    order, order_back = ([step for step in steps if step < blocks] for steps in (ORDER, ORDER_BACK))
     f32 = lambda *shape: jax.ShapeDtypeStruct(shape, jnp.float32)
     scratch = lambda *shape: pltpu.VMEM(shape, jnp.float32)
     split = lambda count: pltpu.VMEM(((blocks + 1) * count, 6 * rows), jnp.bfloat16)
@@ -301,25 +306,28 @@
         [jax.ShapeDtypeStruct((6 * rows, 2 * rows), jnp.bfloat16), f32(blocks + 1, rows), f32(blocks + 1, rows), f32(size, rows)],
         [],
     )
-    spec, keep, swap = call(
+    swap = lambda part: lax.ppermute(part, "dp", [(0, 1), (1, 0)])
+    other_taps = swap(call(functools.partial(gather_kernel, order, half), "gather", arrived, [f32(blocks, half, rows)], [])[0])
+    spec, keep, partial_sum = call(
         functools.partial(analyse_kernel, order, half, np.float32(scale)),
         "analyse",
         [*arrived, *tables],
-        [f32((blocks + 1) * size, 2 * rows), f32(blocks, half, rows), f32(2, blocks, half, rows)],
+        [f32((blocks + 1) * size, 2 * rows), f32(blocks, half, rows), f32(blocks, half, rows)],
         [held, split(size), split(2 * half), scratch((blocks + 1) * 2 * half, 2 * rows)],
     )
-    swapped = lax.ppermute(swap, "dp", [(0, 1), (1, 0)])
-    leaving = call(
-        functools.partial(combine_kernel, order, half),
+    partial_sum = swap(partial_sum)
+    [both] = call(
+        functools.partial(combine_kernel, blocks, half),
         "combine",
-        [spec, keep, swapped, *tables],
-        [f32(size, rows)] * blocks,
-        [held, split(half), scratch((blocks + 1) * half, 2 * rows), split(4 * half), scratch((blocks + 1) * 4 * half, 2 * rows)],
-    )
-    arrived = exchange(leaving, order)
+        [spec, other_taps, *tables],
+        [f32(blocks, 4 * half, rows)],
+        [split(half), scratch((blocks + 1) * half, 2 * rows), split(4 * half), scratch((blocks + 1) * 4 * half, 2 * rows)],
+    )
+    leaving = call(functools.partial(finish_kernel, order_back, half), "finish", [both, keep, partial_sum], [f32(size, rows)] * blocks, [])
+    arrived = exchange(leaving, order_back)
     wide = jax.ShapeDtypeStruct((rows, channels), jnp.bfloat16)
     return call(
-        functools.partial(unpack_kernel, order, half),
+        functools.partial(unpack_kernel, order_back, half),
         "unpack",
         [*arrived, gate, upstream],
         [wide, wide, wide, f32(rows, channels // 2)],

time: 44.8 us -> 41.7 us (0.931)
  waiting for transfers between devices: 12.4 us -> 7.92 us
  starting transfers between devices: 24.2 us -> 27.3 us
  local copies, waits for them, and re-layouts: 0.89 us -> 0.01 us
  Pallas kernels: 6.42 us -> 5.65 us
    ppermute x14, waiting for transfers between devices: 10.9 us -> 7.92 us  [exchange(): lax.ppermute(part, 'context', [(place, place ^ step) for place in range(d...]
    ppermute x14, starting transfers between devices: 24.2 us -> 26.6 us  [exchange(): lax.ppermute(part, 'context', [(place, place ^ step) for place in range(d...]
    ppermute x1 -> x2, waiting for transfers between devices: 1.52 us -> 0.01 us  [tiled_shards(): swap = lambda part: lax.ppermute(part, 'dp', [(0, 1), (1, 0)])]
    unnamed x6 -> x4, local copies, waits for them, and re-layouts: 0.89 us -> 0.01 us
    pallas_call x5 -> x7, Pallas kernels: 6.42 us -> 5.65 us  [call(): pl.pallas_call(kernel, out_shape=outputs, in_specs=[pl.BlockSpec(memory_s...]
    ppermute x1 -> x2, starting transfers between devices: 0.08 us -> 0.63 us  [tiled_shards(): swap = lambda part: lax.ppermute(part, 'dp', [(0, 1), (1, 0)])]
  transfers between devices with their start and end apart: 15 -> 16, of which waited for: 9 -> 4; matrix products, arithmetic and copies ran while one was open for 0% -> 0% of each run, Pallas kernels for 1% -> 8%
where the time goes in v2:
time: 41.7 us; the launch traced here: 41.6 us
  starting transfers between devices  27.3 us (65%)
  waiting for transfers between devices  7.92 us (19%)
  Pallas kernels  5.65 us (14%)
  between operations  0.72 us (2%)
    ppermute x14, starting transfers between devices, exchange(): lax.ppermute(part, 'context', [(place, place ^ step) for place in range(d...  26.6 us
    ppermute x14, waiting for transfers between devices, exchange(): lax.ppermute(part, 'context', [(place, place ^ step) for place in range(d...  7.92 us
    pallas_call x7, Pallas kernels, call(): pl.pallas_call(kernel, out_shape=outputs, in_specs=[pl.BlockSpec(memory_s...  5.65 us
  transfers between devices with their start and end apart: 16, of which 4 were waited for; matrix products, arithmetic and copies ran while one was open for 0% of the time, Pallas kernels for 8%

profile of v2, /device:TPU:0, one launch (start us, length us, event | category | flops | bytes accessed | tf_op | source)
XLA Modules:
  0.0 41.6 jit_solution(16203586728750232495)
XLA Ops:
  0.6 1.4 %pack.1 = (f32[160,128]{1,0:T(8,128)S(1)}, f32[160,128]{1,0:T(8,128)S(1)}, f32[160,128]{1,0:T(8,128)S(1)}, f32[160,128]{1,0:T(8,128)S(1)}, f32[160,128]{1,0:T(8,...) custom-call(bf16[128,512]{1,0:T(8,128)(2,1)} %bitcast.10, ...), custom_call_target="tpu_custom_call" | custom-call | tf_op jit(solution)/shard_map/pack/pallas_call | solution.py:279
  2.0 4.1 %collective-permute-start = (f32[160,128]{1,0:T(8,128)S(1)}, f32[160,128]{1,0:T(8,128)S(1)}, u32[]{:S(2)}, u32[]{:S(2)}) collective-permute-start(f32[160,128]{1,0:T(8,128)S(1)} %get-tuple-element.31), channel_id=1, source_target_pairs={{0,8},{2,10},{4,12},{6,14},{8,0},{10,2},{12,4},{14,6},{1,9},{3,11}... | collective-permute-start | bytes 245768 | tf_op jit(solution)/shard_map/ppermute | solution.py:267
  6.1 2.5 %collective-permute-start.1 = (f32[160,128]{1,0:T(8,128)S(1)}, f32[160,128]{1,0:T(8,128)S(1)}, u32[]{:S(2)}, u32[]{:S(2)}) collective-permute-start(f32[160,128]{1,0:T(8,128)S(1)} %get-tuple-element.32), channel_id=1, source_target_pairs={{0,6},{2,4},{4,2},{6,0},{8,14},{10,12},{12,10},{14,8},{1,7},{3,5},... | collective-permute-start | bytes 245768 | tf_op jit(solution)/shard_map/ppermute | solution.py:267
  8.7 0.3 collective-permute-start.2
  8.9 3.4 %collective-permute-start.3 = (f32[160,128]{1,0:T(8,128)S(1)}, f32[160,128]{1,0:T(8,128)S(1)}, u32[]{:S(2)}, u32[]{:S(2)}) collective-permute-start(f32[160,128]{1,0:T(8,128)S(1)} %get-tuple-element.34), channel_id=1, source_target_pairs={{0,14},{2,12},{4,10},{6,8},{8,6},{10,4},{12,2},{14,0},{1,15},{3,13... | collective-permute-start | bytes 245768 | tf_op jit(solution)/shard_map/ppermute | solution.py:267
  12.4 0.7 %collective-permute-start.4 = (f32[160,128]{1,0:T(8,128)S(1)}, f32[160,128]{1,0:T(8,128)S(1)}, u32[]{:S(2)}, u32[]{:S(2)}) collective-permute-start(f32[160,128]{1,0:T(8,128)S(1)} %get-tuple-element.35), channel_id=1, source_target_pairs={{0,4},{2,6},{4,0},{6,2},{8,12},{10,14},{12,8},{14,10},{1,5},{3,7},... | collective-permute-start | bytes 245768 | tf_op jit(solution)/shard_map/ppermute | solution.py:267
  13.1 0.0 collective-permute-done._.refs_0_
  13.1 2.0 %collective-permute-start.5 = (f32[160,128]{1,0:T(8,128)S(1)}, f32[160,128]{1,0:T(8,128)S(1)}, u32[]{:S(2)}, u32[]{:S(2)}) collective-permute-start(f32[160,128]{1,0:T(8,128)S(1)} %get-tuple-element.36), channel_id=1, source_target_pairs={{0,12},{2,14},{4,8},{6,10},{8,4},{10,6},{12,0},{14,2},{1,13},{3,15... | collective-permute-start | bytes 245768 | tf_op jit(solution)/shard_map/ppermute | solution.py:267
  15.0 0.0 collective-permute-done.1.refs_1_
  15.1 1.4 %collective-permute-start.6 = (f32[160,128]{1,0:T(8,128)S(1)}, f32[160,128]{1,0:T(8,128)S(1)}, u32[]{:S(2)}, u32[]{:S(2)}) collective-permute-start(f32[160,128]{1,0:T(8,128)S(1)} %get-tuple-element.37), channel_id=1, source_target_pairs={{0,2},{2,0},{4,6},{6,4},{8,10},{10,8},{12,14},{14,12},{1,3},{3,1},... | collective-permute-start | bytes 245768 | tf_op jit(solution)/shard_map/ppermute | solution.py:267
  16.4 0.3 tables.1
  16.8 1.8 %collective-permute-done.2.refs_2_ = f32[160,128]{1,0:T(8,128)S(1)} collective-permute-done((f32[160,128]{1,0:T(8,128)S(1)}, f32[160,128]{1,0:T(8,128)S(1)}, u32[]{:S(2)}, u32[]{:S(2)}) %collective-permute-start.2) | collective-permute-done | bytes 81952 | tf_op jit(solution)/shard_map/ppermute | solution.py:267
  18.6 0.0 collective-permute-done.3.refs_3_
  18.6 1.1 %collective-permute-done.4.refs_4_ = f32[160,128]{1,0:T(8,128)S(1)} collective-permute-done((f32[160,128]{1,0:T(8,128)S(1)}, f32[160,128]{1,0:T(8,128)S(1)}, u32[]{:S(2)}, u32[]{:S(2)}) %collective-permute-start.4) | collective-permute-done | bytes 81952 | tf_op jit(solution)/shard_map/ppermute | solution.py:267
  19.7 0.0 collective-permute-done.5.refs_5_
  19.7 0.0 collective-permute-done.6.refs_6_
  19.8 0.1 collective-permute-start.7
  19.9 1.6 %analyse.1 = (f32[1440,256]{1,0:T(8,128)S(1)}, f32[8,32,128]{2,1,0:T(8,128)S(1)}, f32[8,32,128]{2,1,0:T(8,128)S(1)}) custom-call(f32[160,128]{1,0:T(8,128)S(1)} %collective-permute-done._.refs_0_, f32[160,128]{1,0:T(8,128)S(1)} %collective-permute-done.1.refs_1_, f32[160,128]{1,0:T(8,128)S(1)} %collective-permute-done.2.refs_2_, ...), custom_call_target="tpu_custom_call" | custom-call | tf_op jit(solution)/shard_map/analyse/pallas_call | solution.py:279
  21.5 0.6 %collective-permute-start.8 = (f32[8,32,128]{2,1,0:T(8,128)S(1)}, f32[8,32,128]{2,1,0:T(8,128)S(1)}, u32[]{:S(2)}, u32[]{:S(2)}) collective-permute-start(f32[8,32,128]{2,1,0:T(8,128)S(1)} %get-tuple-element.45), channel_id=1, source_target_pairs={{0,1},{1,0},{2,3},{3,2},{4,5},{5,4},{6,7},{7,6},{8,9},{9,8},{10,11... | collective-permute-start | bytes 393224 | tf_op jit(solution)/shard_map/ppermute | solution.py:309
  22.0 0.0 collective-permute-done.7.swapped_ref
  22.0 0.0 copy-start
  22.0 0.0 copy-start.1
  22.0 1.2 %combine.1.held_ref = f32[8,128,128]{2,1,0:T(8,128)S(1)} custom-call(f32[1440,256]{1,0:T(8,128)S(1)} %get-tuple-element.43.spec_ref, f32[8,32,128]{2,1,0:T(8,128)S(1)} %collective-permute-done.7.swapped_ref, bf16[768,256]{1,0:T(8,128)(2,1)S(1)} %get-tuple-element.40.refs_8_.table_ref, f32[9,128]{1,0:T(8,128)S(1)} %get-tuple-element.41.refs_9_.cos_ref, ...), custom_call_target="tpu_custom_call" | custom-call | tf_op jit(solution)/shard_map/combine/pallas_call | solution.py:279
  23.3 0.0 collective-permute-done.8.swapped_ref
  23.3 0.1 finish.1
  23.3 3.9 %collective-permute-start.9 = (f32[160,128]{1,0:T(8,128)S(1)}, f32[160,128]{1,0:T(8,128)S(1)}, u32[]{:S(2)}, u32[]{:S(2)}) collective-permute-start(f32[160,128]{1,0:T(8,128)S(1)} %get-tuple-element.46), channel_id=1, source_target_pairs={{0,8},{2,10},{4,12},{6,14},{8,0},{10,2},{12,4},{14,6},{1,9},{3,11}... | collective-permute-start | bytes 245768 | tf_op jit(solution)/shard_map/ppermute | solution.py:267
  27.2 0.0 collective-permute-start.10
  27.2 2.7 %collective-permute-start.11 = (f32[160,128]{1,0:T(8,128)S(1)}, f32[160,128]{1,0:T(8,128)S(1)}, u32[]{:S(2)}, u32[]{:S(2)}) collective-permute-start(f32[160,128]{1,0:T(8,128)S(1)} %get-tuple-element.48), channel_id=1, source_target_pairs={{0,10},{2,8},{4,14},{6,12},{8,2},{10,0},{12,6},{14,4},{1,11},{3,9}... | collective-permute-start | bytes 245768 | tf_op jit(solution)/shard_map/ppermute | solution.py:267
  29.9 3.5 %collective-permute-start.12 = (f32[160,128]{1,0:T(8,128)S(1)}, f32[160,128]{1,0:T(8,128)S(1)}, u32[]{:S(2)}, u32[]{:S(2)}) collective-permute-start(f32[160,128]{1,0:T(8,128)S(1)} %get-tuple-element.49), channel_id=1, source_target_pairs={{0,14},{2,12},{4,10},{6,8},{8,6},{10,4},{12,2},{14,0},{1,15},{3,13... | collective-permute-start | bytes 245768 | tf_op jit(solution)/shard_map/ppermute | solution.py:267
  33.4 0.0 collective-permute-start.13
  33.4 0.0 collective-permute-done.9.refs_0_
  33.4 1.3 %collective-permute-start.14 = (f32[160,128]{1,0:T(8,128)S(1)}, f32[160,128]{1,0:T(8,128)S(1)}, u32[]{:S(2)}, u32[]{:S(2)}) collective-permute-start(f32[160,128]{1,0:T(8,128)S(1)} %get-tuple-element.51), channel_id=1, source_target_pairs={{0,12},{2,14},{4,8},{6,10},{8,4},{10,6},{12,0},{14,2},{1,13},{3,15... | collective-permute-start | bytes 245768 | tf_op jit(solution)/shard_map/ppermute | solution.py:267
  34.7 0.0 collective-permute-done.10.refs_1_
  34.7 0.9 %collective-permute-start.15 = (f32[160,128]{1,0:T(8,128)S(1)}, f32[160,128]{1,0:T(8,128)S(1)}, u32[]{:S(2)}, u32[]{:S(2)}) collective-permute-start(f32[160,128]{1,0:T(8,128)S(1)} %get-tuple-element.52), channel_id=1, source_target_pairs={{0,2},{2,0},{4,6},{6,4},{8,10},{10,8},{12,14},{14,12},{1,3},{3,1},... | collective-permute-start | bytes 245768 | tf_op jit(solution)/shard_map/ppermute | solution.py:267
  35.6 3.3 %collective-permute-done.11.refs_2_ = f32[160,128]{1,0:T(8,128)S(1)} collective-permute-done((f32[160,128]{1,0:T(8,128)S(1)}, f32[160,128]{1,0:T(8,128)S(1)}, u32[]{:S(2)}, u32[]{:S(2)}) %collective-permute-start.11) | collective-permute-done | bytes 81952 | tf_op jit(solution)/shard_map/ppermute | solution.py:267
  38.9 0.0 collective-permute-done.12.refs_3_
  38.9 1.6 %collective-permute-done.13.refs_4_ = f32[160,128]{1,0:T(8,128)S(1)} collective-permute-done((f32[160,128]{1,0:T(8,128)S(1)}, f32[160,128]{1,0:T(8,128)S(1)}, u32[]{:S(2)}, u32[]{:S(2)}) %collective-permute-start.13) | collective-permute-done | bytes 81952 | tf_op jit(solution)/shard_map/ppermute | solution.py:267
  40.5 0.0 collective-permute-done.14.refs_5_
  40.5 0.0 collective-permute-done.15.refs_6_
  40.5 0.0 copy-done
  40.5 0.0 copy-done.1
  40.5 1.0 %unpack.1 = (bf16[128,512]{1,0:T(8,128)(2,1)}, bf16[128,512]{1,0:T(8,128)(2,1)}, bf16[128,512]{1,0:T(8,128)(2,1)}, f32[128,256]{1,0:T(8,128)}) custom-call(f32[160,128]{1,0:T(8,128)S(1)} %collective-permute-done.9.refs_0_, f32[160,128]{1,0:T(8,128)S(1)} %collective-permute-done.10.refs_1_, f32[160,128]{1,0:T(8,128)S(1)} %collective-permute-done.11.refs_2_, ...), custom_call_target="tpu_custom_call" | custom-call | tf_op jit(solution)/shard_map/unpack/pallas_call | solution.py:279
  (1 shorter events, 0.0 us)
Async XLA Ops:
  2.0 11.0 %collective-permute-start = (f32[160,128]{1,0:T(8,128)S(1)}, f32[160,128]{1,0:T(8,128)S(1)}, u32[]{:S(2)}, u32[]{:S(2)}) collective-permute-start(f32[160,128]{1,0:T(8,128)S(1)} %get-tuple-element.31), channel_id=1, source_target_pairs={{0,8},{2,10},{4,12},{6,14},{8,0},{10,2},{12,4},{14,6},{1,9},{3,11}... | collective-permute-start | bytes 245768 | tf_op jit(solution)/shard_map/ppermute | solution.py:267
  6.1 8.9 %collective-permute-start.1 = (f32[160,128]{1,0:T(8,128)S(1)}, f32[160,128]{1,0:T(8,128)S(1)}, u32[]{:S(2)}, u32[]{:S(2)}) collective-permute-start(f32[160,128]{1,0:T(8,128)S(1)} %get-tuple-element.32), channel_id=1, source_target_pairs={{0,6},{2,4},{4,2},{6,0},{8,14},{10,12},{12,10},{14,8},{1,7},{3,5},... | collective-permute-start | bytes 245768 | tf_op jit(solution)/shard_map/ppermute | solution.py:267
  8.7 9.9 %collective-permute-start.2 = (f32[160,128]{1,0:T(8,128)S(1)}, f32[160,128]{1,0:T(8,128)S(1)}, u32[]{:S(2)}, u32[]{:S(2)}) collective-permute-start(f32[160,128]{1,0:T(8,128)S(1)} %get-tuple-element.33), channel_id=1, source_target_pairs={{0,10},{2,8},{4,14},{6,12},{8,2},{10,0},{12,6},{14,4},{1,11},{3,9}... | collective-permute-start | bytes 245768 | tf_op jit(solution)/shard_map/ppermute | solution.py:267
  8.9 9.7 %collective-permute-start.3 = (f32[160,128]{1,0:T(8,128)S(1)}, f32[160,128]{1,0:T(8,128)S(1)}, u32[]{:S(2)}, u32[]{:S(2)}) collective-permute-start(f32[160,128]{1,0:T(8,128)S(1)} %get-tuple-element.34), channel_id=1, source_target_pairs={{0,14},{2,12},{4,10},{6,8},{8,6},{10,4},{12,2},{14,0},{1,15},{3,13... | collective-permute-start | bytes 245768 | tf_op jit(solution)/shard_map/ppermute | solution.py:267
  12.4 7.4 %collective-permute-start.4 = (f32[160,128]{1,0:T(8,128)S(1)}, f32[160,128]{1,0:T(8,128)S(1)}, u32[]{:S(2)}, u32[]{:S(2)}) collective-permute-start(f32[160,128]{1,0:T(8,128)S(1)} %get-tuple-element.35), channel_id=1, source_target_pairs={{0,4},{2,6},{4,0},{6,2},{8,12},{10,14},{12,8},{14,10},{1,5},{3,7},... | collective-permute-start | bytes 245768 | tf_op jit(solution)/shard_map/ppermute | solution.py:267
  13.1 6.7 %collective-permute-start.5 = (f32[160,128]{1,0:T(8,128)S(1)}, f32[160,128]{1,0:T(8,128)S(1)}, u32[]{:S(2)}, u32[]{:S(2)}) collective-permute-start(f32[160,128]{1,0:T(8,128)S(1)} %get-tuple-element.36), channel_id=1, source_target_pairs={{0,12},{2,14},{4,8},{6,10},{8,4},{10,6},{12,0},{14,2},{1,13},{3,15... | collective-permute-start | bytes 245768 | tf_op jit(solution)/shard_map/ppermute | solution.py:267
  15.1 4.7 %collective-permute-start.6 = (f32[160,128]{1,0:T(8,128)S(1)}, f32[160,128]{1,0:T(8,128)S(1)}, u32[]{:S(2)}, u32[]{:S(2)}) collective-permute-start(f32[160,128]{1,0:T(8,128)S(1)} %get-tuple-element.37), channel_id=1, source_target_pairs={{0,2},{2,0},{4,6},{6,4},{8,10},{10,8},{12,14},{14,12},{1,3},{3,1},... | collective-permute-start | bytes 245768 | tf_op jit(solution)/shard_map/ppermute | solution.py:267
  19.8 2.2 %collective-permute-start.7 = (f32[8,32,128]{2,1,0:T(8,128)S(1)}, f32[8,32,128]{2,1,0:T(8,128)S(1)}, u32[]{:S(2)}, u32[]{:S(2)}) collective-permute-start(f32[8,32,128]{2,1,0:T(8,128)S(1)} %gather.1), channel_id=1, source_target_pairs={{0,1},{1,0},{2,3},{3,2},{4,5},{5,4},{6,7},{7,6},{8,9},{9,8},{10,11... | collective-permute-start | bytes 393224 | tf_op jit(solution)/shard_map/ppermute | solution.py:309
  21.5 1.8 %collective-permute-start.8 = (f32[8,32,128]{2,1,0:T(8,128)S(1)}, f32[8,32,128]{2,1,0:T(8,128)S(1)}, u32[]{:S(2)}, u32[]{:S(2)}) collective-permute-start(f32[8,32,128]{2,1,0:T(8,128)S(1)} %get-tuple-element.45), channel_id=1, source_target_pairs={{0,1},{1,0},{2,3},{3,2},{4,5},{5,4},{6,7},{7,6},{8,9},{9,8},{10,11... | collective-permute-start | bytes 393224 | tf_op jit(solution)/shard_map/ppermute | solution.py:309
  22.0 18.5 %copy-start = (bf16[1,128,512]{2,1,0:T(8,128)(2,1)S(1)}, bf16[1,128,512]{2,1,0:T(8,128)(2,1)}, u32[]{:S(2)}) copy-start(bf16[1,128,512]{2,1,0:T(8,128)(2,1)} %param.5) | copy-start | bytes 393220
  22.0 18.5 %copy-start.1 = (bf16[1,128,512]{2,1,0:T(8,128)(2,1)S(1)}, bf16[1,128,512]{2,1,0:T(8,128)(2,1)}, u32[]{:S(2)}) copy-start(bf16[1,128,512]{2,1,0:T(8,128)(2,1)} %param.7) | copy-start | bytes 393220
  23.3 10.1 %collective-permute-start.9 = (f32[160,128]{1,0:T(8,128)S(1)}, f32[160,128]{1,0:T(8,128)S(1)}, u32[]{:S(2)}, u32[]{:S(2)}) collective-permute-start(f32[160,128]{1,0:T(8,128)S(1)} %get-tuple-element.46), channel_id=1, source_target_pairs={{0,8},{2,10},{4,12},{6,14},{8,0},{10,2},{12,4},{14,6},{1,9},{3,11}... | collective-permute-start | bytes 245768 | tf_op jit(solution)/shard_map/ppermute | solution.py:267
  27.2 7.5 %collective-permute-start.10 = (f32[160,128]{1,0:T(8,128)S(1)}, f32[160,128]{1,0:T(8,128)S(1)}, u32[]{:S(2)}, u32[]{:S(2)}) collective-permute-start(f32[160,128]{1,0:T(8,128)S(1)} %get-tuple-element.47), channel_id=1, source_target_pairs={{0,6},{2,4},{4,2},{6,0},{8,14},{10,12},{12,10},{14,8},{1,7},{3,5},... | collective-permute-start | bytes 245768 | tf_op jit(solution)/shard_map/ppermute | solution.py:267
  27.2 11.7 %collective-permute-start.11 = (f32[160,128]{1,0:T(8,128)S(1)}, f32[160,128]{1,0:T(8,128)S(1)}, u32[]{:S(2)}, u32[]{:S(2)}) collective-permute-start(f32[160,128]{1,0:T(8,128)S(1)} %get-tuple-element.48), channel_id=1, source_target_pairs={{0,10},{2,8},{4,14},{6,12},{8,2},{10,0},{12,6},{14,4},{1,11},{3,9}... | collective-permute-start | bytes 245768 | tf_op jit(solution)/shard_map/ppermute | solution.py:267
  29.9 9.0 %collective-permute-start.12 = (f32[160,128]{1,0:T(8,128)S(1)}, f32[160,128]{1,0:T(8,128)S(1)}, u32[]{:S(2)}, u32[]{:S(2)}) collective-permute-start(f32[160,128]{1,0:T(8,128)S(1)} %get-tuple-element.49), channel_id=1, source_target_pairs={{0,14},{2,12},{4,10},{6,8},{8,6},{10,4},{12,2},{14,0},{1,15},{3,13... | collective-permute-start | bytes 245768 | tf_op jit(solution)/shard_map/ppermute | solution.py:267
  33.4 7.1 %collective-permute-start.13 = (f32[160,128]{1,0:T(8,128)S(1)}, f32[160,128]{1,0:T(8,128)S(1)}, u32[]{:S(2)}, u32[]{:S(2)}) collective-permute-start(f32[160,128]{1,0:T(8,128)S(1)} %get-tuple-element.50), channel_id=1, source_target_pairs={{0,4},{2,6},{4,0},{6,2},{8,12},{10,14},{12,8},{14,10},{1,5},{3,7},... | collective-permute-start | bytes 245768 | tf_op jit(solution)/shard_map/ppermute | solution.py:267
  33.4 7.1 %collective-permute-start.14 = (f32[160,128]{1,0:T(8,128)S(1)}, f32[160,128]{1,0:T(8,128)S(1)}, u32[]{:S(2)}, u32[]{:S(2)}) collective-permute-start(f32[160,128]{1,0:T(8,128)S(1)} %get-tuple-element.51), channel_id=1, source_target_pairs={{0,12},{2,14},{4,8},{6,10},{8,4},{10,6},{12,0},{14,2},{1,13},{3,15... | collective-permute-start | bytes 245768 | tf_op jit(solution)/shard_map/ppermute | solution.py:267
  34.7 5.8 %collective-permute-start.15 = (f32[160,128]{1,0:T(8,128)S(1)}, f32[160,128]{1,0:T(8,128)S(1)}, u32[]{:S(2)}, u32[]{:S(2)}) collective-permute-start(f32[160,128]{1,0:T(8,128)S(1)} %get-tuple-element.52), channel_id=1, source_target_pairs={{0,2},{2,0},{4,6},{6,4},{8,10},{10,8},{12,14},{14,12},{1,3},{3,1},... | collective-permute-start | bytes 245768 | tf_op jit(solution)/shard_map/ppermute | solution.py:267

commit v3 on v2

--- a/solution.py
+++ b/solution.py
@@ -11,9 +11,8 @@
 
 LANES = 128
 LIMIT = 16 * 2**20
-PARTS = 1
 PACK_LIMIT = 53 * 2**20 + 2**18
-ORDER = (4, 3, 5, 7, 2, 6, 1, 0)
+ORDER = (4, 2, 5, 7, 3, 6, 1, 0)
 ORDER_BACK = (4, 3, 5, 7, 2, 6, 1, 0)
 HIGHEST = lax.Precision.HIGHEST
 
@@ -55,11 +54,9 @@
     rows_ref[at, pl.ds(2 * width, width)] = high
 
 
-def multiply(rows_ref, table_ref, out_ref, parts):
-    size = rows_ref.shape[0] // parts
-    for part in range(parts):
-        at = pl.ds(part * size, size)
-        out_ref[at, :] = jnp.dot(rows_ref[at, :], table_ref[...], preferred_element_type=jnp.float32)
+def multiply(rows_ref, table_ref, out_ref, base, size):
+    at = pl.ds(base, size)
+    out_ref[at, :] = jnp.dot(rows_ref[at, :], table_ref[...], preferred_element_type=jnp.float32)
 
 
 def weighted(terms):
@@ -105,9 +102,10 @@
     return sums
 
 
-def forward_rows(blocks, rows, load, cos_ref, sin_ref, rows_ref):
-    for first in range(0, rows, 16):
-        sums = forward_sums(blocks, [load(block, pl.ds(first, 16)) for block in range(blocks)])
+def forward_rows(blocks, sources, load, cos_ref, sin_ref, rows_ref, base):
+    rows = 16 * len(sources)
+    for first, source in zip(range(0, rows, 16), sources):
+        sums = forward_sums(blocks, [load(block, pl.ds(source, 16)) for block in range(blocks)])
         for k in range(blocks + 1):
             real, imag = sums[k]
             if k > 0:
@@ -117,7 +115,7 @@
                 else:
                     real, imag = real * cosine + imag * sine, imag * cosine - real * sine
             imag = jnp.zeros_like(real) if imag is None else imag
-            store_split(rows_ref, pl.ds(k * rows + first, 16), jnp.concatenate([real, imag], axis=1))
+            store_split(rows_ref, pl.ds(base + k * rows + first, 16), jnp.concatenate([real, imag], axis=1))
 
 
 def times(first, second, conjugate):
@@ -126,13 +124,13 @@
     return jnp.concatenate([real, imag], axis=1)
 
 
-def inverse_sums(blocks, rows, back_ref, cos_ref, sin_ref, put):
+def inverse_sums(blocks, rows, back_ref, base, cos_ref, sin_ref, put):
     turn = math.pi / blocks
     scale = 1.0 / (2 * blocks * LANES)
     for first in range(0, rows, 8):
         real, imag = [], [None] * (blocks + 1)
         for k in range(blocks + 1):
-            at = pl.ds(k * rows + first, 8)
+            at = pl.ds(base + k * rows + first, 8)
             weight = np.float32(scale if k in (0, blocks) else 2.0 * scale)
             one = back_ref[at, pl.ds(0, LANES)] * weight
             if k > 0:
@@ -159,44 +157,66 @@
 
 
 def analyse_kernel(order, half, scale, *refs):
-    blocks, size = len(order), 5 * half
+    blocks = len(order)
     block_refs, (table_ref, cos_ref, sin_ref, spec_ref, keep_ref, swap_ref, held_ref, in_ref, out_ref, back_ref) = refs[:blocks], refs[blocks:]
     me = lax.axis_index("context")
     for step, block_ref in zip(order, block_refs):
         held_ref[me ^ step] = block_ref[...]
-    forward_rows(blocks, size, lambda block, at: held_ref[block, at, :], cos_ref, sin_ref, in_ref)
-    multiply(in_ref, table_ref, spec_ref, PARTS)
-    for k in range(blocks + 1):
-        for first in range(0, 2 * half, 16):
-            at = lambda part: pl.ds(k * size + 2 * half * part + first, 16)
-            store_split(out_ref, pl.ds(k * 2 * half + first, 16), times(spec_ref[at(1), :], spec_ref[at(0), :], True) * scale)
-    multiply(out_ref, table_ref, back_ref, PARTS)
-
-    def put(block, first, value):
-        if first < half:
-            keep_ref[block, pl.ds(first, 8), :] = value
-        else:
-            swap_ref[block, pl.ds(first - half, 8), :] = value
-
-    inverse_sums(blocks, 2 * half, back_ref, cos_ref, sin_ref, put)
+    load = lambda block, at: held_ref[block, at, :]
+    cells = (blocks + 1) * half
+
+    def forward(group):
+        starts = [4 * half] if group == 2 else [group * half, (2 + group) * half]
+        sources = [start + row for start in starts for row in range(0, half, 16)]
+        forward_rows(blocks, sources, load, cos_ref, sin_ref, in_ref, 2 * group * cells)
+        multiply(in_ref, table_ref, spec_ref, 2 * group * cells, len(starts) * cells)
+
+    def back(group):
+        for k in range(blocks + 1):
+            for first in range(0, half, 16):
+                at = lambda part: pl.ds(2 * group * cells + (2 * k + part) * half + first, 16)
+                store_split(out_ref, pl.ds(group * cells + k * half + first, 16), times(spec_ref[at(1), :], spec_ref[at(0), :], True) * scale)
+        multiply(out_ref, table_ref, back_ref, group * cells, cells)
+
+    def finish(group, to_ref):
+        def put(block, first, value):
+            to_ref[block, pl.ds(first, 8), :] = value
+
+        inverse_sums(blocks, half, back_ref, group * cells, cos_ref, sin_ref, put)
+
+    forward(1)
+    forward(0)
+    back(1)
+    forward(2)
+    back(0)
+    finish(1, swap_ref)
+    finish(0, keep_ref)
 
 
 def combine_kernel(blocks, half, spec_ref, swapped_ref, table_ref, cos_ref, sin_ref, held_ref, in_ref, taps_ref, out_ref, back_ref):
-    size = 5 * half
-    forward_rows(blocks, half, lambda block, at: swapped_ref[block, at, :], cos_ref, sin_ref, in_ref)
-    multiply(in_ref, table_ref, taps_ref, 1)
-    for k in range(blocks + 1):
-        for first in range(0, 2 * half, 16):
-            taps = spec_ref[pl.ds(k * size + 4 * half + first, 16), :] if first < half else taps_ref[pl.ds(k * half + first - half, 16), :]
-            for part in range(2):
-                spec = spec_ref[pl.ds(k * size + 2 * half * part + first, 16), :]
-                store_split(out_ref, pl.ds(k * 4 * half + 2 * half * part + first, 16), times(spec, taps, part == 1))
-    multiply(out_ref, table_ref, back_ref, PARTS)
-
-    def put(block, first, value):
-        held_ref[block, pl.ds(first, 8), :] = value
-
-    inverse_sums(blocks, 4 * half, back_ref, cos_ref, sin_ref, put)
+    cells = (blocks + 1) * half
+
+    def back(group, taps_at):
+        for k in range(blocks + 1):
+            for first in range(0, half, 16):
+                taps = taps_at(k * half + first)
+                for part in range(2):
+                    at = pl.ds(2 * group * cells + (2 * k + part) * half + first, 16)
+                    store_split(out_ref, at, times(spec_ref[at, :], taps, part == 1))
+        multiply(out_ref, table_ref, back_ref, 2 * group * cells, 2 * cells)
+
+    def finish(group):
+        def put(block, first, value):
+            held_ref[block, pl.ds((2 * (first // half) + group) * half + first % half, 8), :] = value
+
+        inverse_sums(blocks, 2 * half, back_ref, 2 * group * cells, cos_ref, sin_ref, put)
+
+    forward_rows(blocks, range(0, half, 16), lambda block, at: swapped_ref[block, at, :], cos_ref, sin_ref, in_ref, 0)
+    multiply(in_ref, table_ref, taps_ref, 0, cells)
+    back(0, lambda row: spec_ref[pl.ds(4 * cells + row, 16), :])
+    back(1, lambda row: taps_ref[pl.ds(row, 16), :])
+    finish(0)
+    finish(1)
 
 
 def finish_kernel(order, half, held_ref, keep_ref, swapped_ref, *block_refs):

time: 41.7 us -> 41.1 us (0.986)
  starting transfers between devices: 27.3 us -> 26.3 us
  waiting for transfers between devices: 7.92 us -> 8.84 us
  Pallas kernels: 5.65 us -> 5.04 us
    ppermute x14, starting transfers between devices: 26.6 us -> 25.7 us  [exchange(): lax.ppermute(part, 'context', [(place, place ^ step) for place in range(d...]
    ppermute x14, waiting for transfers between devices: 7.92 us -> 8.81 us  [exchange(): lax.ppermute(part, 'context', [(place, place ^ step) for place in range(d...]
    pallas_call x7, Pallas kernels: 5.65 us -> 5.04 us  [call(): pl.pallas_call(kernel, out_shape=outputs, in_specs=[pl.BlockSpec(memory_s...]
  transfers between devices with their start and end apart: 16 -> 16, of which waited for: 4 -> 5; matrix products, arithmetic and copies ran while one was open for 0% -> 0% of each run, Pallas kernels for 8% -> 6%
where the time goes in v3:
time: 41.1 us; the launch traced here: 40.9 us
  starting transfers between devices  26.3 us (64%)
  waiting for transfers between devices  8.84 us (22%)
  Pallas kernels  5.04 us (12%)
  between operations  0.71 us (2%)
    ppermute x14, starting transfers between devices, exchange(): lax.ppermute(part, 'context', [(place, place ^ step) for place in range(d...  25.7 us
    ppermute x14, waiting for transfers between devices, exchange(): lax.ppermute(part, 'context', [(place, place ^ step) for place in range(d...  8.81 us
    pallas_call x7, Pallas kernels, call(): pl.pallas_call(kernel, out_shape=outputs, in_specs=[pl.BlockSpec(memory_s...  5.04 us
  transfers between devices with their start and end apart: 16, of which 5 were waited for; matrix products, arithmetic and copies ran while one was open for 0% of the time, Pallas kernels for 6%

profile of v3, /device:TPU:0, one launch (start us, length us, event | category | flops | bytes accessed | tf_op | source)
XLA Modules:
  0.0 40.9 jit_solution(11892090562462693330)
XLA Ops:
  0.6 1.4 %pack.1 = (f32[160,128]{1,0:T(8,128)S(1)}, f32[160,128]{1,0:T(8,128)S(1)}, f32[160,128]{1,0:T(8,128)S(1)}, f32[160,128]{1,0:T(8,128)S(1)}, f32[160,128]{1,0:T(8,...) custom-call(bf16[128,512]{1,0:T(8,128)(2,1)} %bitcast.10, ...), custom_call_target="tpu_custom_call" | custom-call | tf_op jit(solution)/shard_map/pack/pallas_call | solution.py:299
  2.0 4.1 %collective-permute-start = (f32[160,128]{1,0:T(8,128)S(1)}, f32[160,128]{1,0:T(8,128)S(1)}, u32[]{:S(2)}, u32[]{:S(2)}) collective-permute-start(f32[160,128]{1,0:T(8,128)S(1)} %get-tuple-element.31), channel_id=1, source_target_pairs={{0,8},{2,10},{4,12},{6,14},{8,0},{10,2},{12,4},{14,6},{1,9},{3,11}... | collective-permute-start | bytes 245768 | tf_op jit(solution)/shard_map/ppermute | solution.py:287
  6.1 1.6 %collective-permute-start.1 = (f32[160,128]{1,0:T(8,128)S(1)}, f32[160,128]{1,0:T(8,128)S(1)}, u32[]{:S(2)}, u32[]{:S(2)}) collective-permute-start(f32[160,128]{1,0:T(8,128)S(1)} %get-tuple-element.32), channel_id=1, source_target_pairs={{0,4},{2,6},{4,0},{6,2},{8,12},{10,14},{12,8},{14,10},{1,5},{3,7},... | collective-permute-start | bytes 245768 | tf_op jit(solution)/shard_map/ppermute | solution.py:287
  7.7 1.3 %collective-permute-start.2 = (f32[160,128]{1,0:T(8,128)S(1)}, f32[160,128]{1,0:T(8,128)S(1)}, u32[]{:S(2)}, u32[]{:S(2)}) collective-permute-start(f32[160,128]{1,0:T(8,128)S(1)} %get-tuple-element.33), channel_id=1, source_target_pairs={{0,10},{2,8},{4,14},{6,12},{8,2},{10,0},{12,6},{14,4},{1,11},{3,9}... | collective-permute-start | bytes 245768 | tf_op jit(solution)/shard_map/ppermute | solution.py:287
  9.0 2.4 %collective-permute-start.3 = (f32[160,128]{1,0:T(8,128)S(1)}, f32[160,128]{1,0:T(8,128)S(1)}, u32[]{:S(2)}, u32[]{:S(2)}) collective-permute-start(f32[160,128]{1,0:T(8,128)S(1)} %get-tuple-element.34), channel_id=1, source_target_pairs={{0,14},{2,12},{4,10},{6,8},{8,6},{10,4},{12,2},{14,0},{1,15},{3,13... | collective-permute-start | bytes 245768 | tf_op jit(solution)/shard_map/ppermute | solution.py:287
  11.4 1.6 %collective-permute-start.4 = (f32[160,128]{1,0:T(8,128)S(1)}, f32[160,128]{1,0:T(8,128)S(1)}, u32[]{:S(2)}, u32[]{:S(2)}) collective-permute-start(f32[160,128]{1,0:T(8,128)S(1)} %get-tuple-element.35), channel_id=1, source_target_pairs={{0,6},{2,4},{4,2},{6,0},{8,14},{10,12},{12,10},{14,8},{1,7},{3,5},... | collective-permute-start | bytes 245768 | tf_op jit(solution)/shard_map/ppermute | solution.py:287
  13.1 0.0 collective-permute-done._.refs_0_
  13.1 1.8 %collective-permute-start.5 = (f32[160,128]{1,0:T(8,128)S(1)}, f32[160,128]{1,0:T(8,128)S(1)}, u32[]{:S(2)}, u32[]{:S(2)}) collective-permute-start(f32[160,128]{1,0:T(8,128)S(1)} %get-tuple-element.36), channel_id=1, source_target_pairs={{0,12},{2,14},{4,8},{6,10},{8,4},{10,6},{12,0},{14,2},{1,13},{3,15... | collective-permute-start | bytes 245768 | tf_op jit(solution)/shard_map/ppermute | solution.py:287
  14.8 0.0 collective-permute-done.1.refs_1_
  14.8 1.5 %collective-permute-start.6 = (f32[160,128]{1,0:T(8,128)S(1)}, f32[160,128]{1,0:T(8,128)S(1)}, u32[]{:S(2)}, u32[]{:S(2)}) collective-permute-start(f32[160,128]{1,0:T(8,128)S(1)} %get-tuple-element.37), channel_id=1, source_target_pairs={{0,2},{2,0},{4,6},{6,4},{8,10},{10,8},{12,14},{14,12},{1,3},{3,1},... | collective-permute-start | bytes 245768 | tf_op jit(solution)/shard_map/ppermute | solution.py:287
  16.4 0.3 tables.1
  16.7 1.7 %collective-permute-done.2.refs_2_ = f32[160,128]{1,0:T(8,128)S(1)} collective-permute-done((f32[160,128]{1,0:T(8,128)S(1)}, f32[160,128]{1,0:T(8,128)S(1)}, u32[]{:S(2)}, u32[]{:S(2)}) %collective-permute-start.2) | collective-permute-done | bytes 81952 | tf_op jit(solution)/shard_map/ppermute | solution.py:287
  18.4 0.0 collective-permute-done.3.refs_3_
  18.4 1.2 %collective-permute-done.4.refs_4_ = f32[160,128]{1,0:T(8,128)S(1)} collective-permute-done((f32[160,128]{1,0:T(8,128)S(1)}, f32[160,128]{1,0:T(8,128)S(1)}, u32[]{:S(2)}, u32[]{:S(2)}) %collective-permute-start.4) | collective-permute-done | bytes 81952 | tf_op jit(solution)/shard_map/ppermute | solution.py:287
  19.6 0.0 collective-permute-done.5.refs_5_
  19.7 0.0 collective-permute-done.6.refs_6_
  19.7 0.1 collective-permute-start.7
  19.8 1.3 %analyse.1 = (f32[1440,256]{1,0:T(8,128)S(1)}, f32[8,32,128]{2,1,0:T(8,128)S(1)}, f32[8,32,128]{2,1,0:T(8,128)S(1)}) custom-call(f32[160,128]{1,0:T(8,128)S(1)} %collective-permute-done._.refs_0_, f32[160,128]{1,0:T(8,128)S(1)} %collective-permute-done.1.refs_1_, f32[160,128]{1,0:T(8,128)S(1)} %collective-permute-done.2.refs_2_, ...), custom_call_target="tpu_custom_call" | custom-call | tf_op jit(solution)/shard_map/analyse/pallas_call | solution.py:299
  21.0 0.6 %collective-permute-start.8 = (f32[8,32,128]{2,1,0:T(8,128)S(1)}, f32[8,32,128]{2,1,0:T(8,128)S(1)}, u32[]{:S(2)}, u32[]{:S(2)}) collective-permute-start(f32[8,32,128]{2,1,0:T(8,128)S(1)} %get-tuple-element.45), channel_id=1, source_target_pairs={{0,1},{1,0},{2,3},{3,2},{4,5},{5,4},{6,7},{7,6},{8,9},{9,8},{10,11... | collective-permute-start | bytes 393224 | tf_op jit(solution)/shard_map/ppermute | solution.py:329
  21.6 0.0 collective-permute-done.7.swapped_ref
  21.6 0.0 copy-start
  21.6 0.0 copy-start.1
  21.6 0.9 %combine.1.held_ref = f32[8,128,128]{2,1,0:T(8,128)S(1)} custom-call(f32[1440,256]{1,0:T(8,128)S(1)} %get-tuple-element.43.spec_ref, f32[8,32,128]{2,1,0:T(8,128)S(1)} %collective-permute-done.7.swapped_ref, bf16[768,256]{1,0:T(8,128)(2,1)S(1)} %get-tuple-element.40.refs_8_.table_ref, f32[9,128]{1,0:T(8,128)S(1)} %get-tuple-element.41.refs_9_.cos_ref, ...), custom_call_target="tpu_custom_call" | custom-call | tf_op jit(solution)/shard_map/combine/pallas_call | solution.py:299
  22.5 0.0 collective-permute-done.8.swapped_ref
  22.6 0.1 finish.1
  22.6 3.9 %collective-permute-start.9 = (f32[160,128]{1,0:T(8,128)S(1)}, f32[160,128]{1,0:T(8,128)S(1)}, u32[]{:S(2)}, u32[]{:S(2)}) collective-permute-start(f32[160,128]{1,0:T(8,128)S(1)} %get-tuple-element.46), channel_id=1, source_target_pairs={{0,8},{2,10},{4,12},{6,14},{8,0},{10,2},{12,4},{14,6},{1,9},{3,11}... | collective-permute-start | bytes 245768 | tf_op jit(solution)/shard_map/ppermute | solution.py:287
  26.5 0.0 collective-permute-start.10
  26.6 2.9 %collective-permute-start.11 = (f32[160,128]{1,0:T(8,128)S(1)}, f32[160,128]{1,0:T(8,128)S(1)}, u32[]{:S(2)}, u32[]{:S(2)}) collective-permute-start(f32[160,128]{1,0:T(8,128)S(1)} %get-tuple-element.48), channel_id=1, source_target_pairs={{0,10},{2,8},{4,14},{6,12},{8,2},{10,0},{12,6},{14,4},{1,11},{3,9}... | collective-permute-start | bytes 245768 | tf_op jit(solution)/shard_map/ppermute | solution.py:287
  29.4 3.4 %collective-permute-start.12 = (f32[160,128]{1,0:T(8,128)S(1)}, f32[160,128]{1,0:T(8,128)S(1)}, u32[]{:S(2)}, u32[]{:S(2)}) collective-permute-start(f32[160,128]{1,0:T(8,128)S(1)} %get-tuple-element.49), channel_id=1, source_target_pairs={{0,14},{2,12},{4,10},{6,8},{8,6},{10,4},{12,2},{14,0},{1,15},{3,13... | collective-permute-start | bytes 245768 | tf_op jit(solution)/shard_map/ppermute | solution.py:287
  32.8 0.0 collective-permute-start.13
  32.8 0.0 collective-permute-done.9.refs_0_
  32.8 0.6 %collective-permute-start.14 = (f32[160,128]{1,0:T(8,128)S(1)}, f32[160,128]{1,0:T(8,128)S(1)}, u32[]{:S(2)}, u32[]{:S(2)}) collective-permute-start(f32[160,128]{1,0:T(8,128)S(1)} %get-tuple-element.51), channel_id=1, source_target_pairs={{0,12},{2,14},{4,8},{6,10},{8,4},{10,6},{12,0},{14,2},{1,13},{3,15... | collective-permute-start | bytes 245768 | tf_op jit(solution)/shard_map/ppermute | solution.py:287
  33.4 1.3 %collective-permute-done.10.refs_1_ = f32[160,128]{1,0:T(8,128)S(1)} collective-permute-done((f32[160,128]{1,0:T(8,128)S(1)}, f32[160,128]{1,0:T(8,128)S(1)}, u32[]{:S(2)}, u32[]{:S(2)}) %collective-permute-start.10) | collective-permute-done | bytes 81952 | tf_op jit(solution)/shard_map/ppermute | solution.py:287
  34.7 0.6 %collective-permute-start.15 = (f32[160,128]{1,0:T(8,128)S(1)}, f32[160,128]{1,0:T(8,128)S(1)}, u32[]{:S(2)}, u32[]{:S(2)}) collective-permute-start(f32[160,128]{1,0:T(8,128)S(1)} %get-tuple-element.52), channel_id=1, source_target_pairs={{0,2},{2,0},{4,6},{6,4},{8,10},{10,8},{12,14},{14,12},{1,3},{3,1},... | collective-permute-start | bytes 245768 | tf_op jit(solution)/shard_map/ppermute | solution.py:287
  35.3 2.7 %collective-permute-done.11.refs_2_ = f32[160,128]{1,0:T(8,128)S(1)} collective-permute-done((f32[160,128]{1,0:T(8,128)S(1)}, f32[160,128]{1,0:T(8,128)S(1)}, u32[]{:S(2)}, u32[]{:S(2)}) %collective-permute-start.11) | collective-permute-done | bytes 81952 | tf_op jit(solution)/shard_map/ppermute | solution.py:287
  38.0 0.0 collective-permute-done.12.refs_3_
  38.0 1.8 %collective-permute-done.13.refs_4_ = f32[160,128]{1,0:T(8,128)S(1)} collective-permute-done((f32[160,128]{1,0:T(8,128)S(1)}, f32[160,128]{1,0:T(8,128)S(1)}, u32[]{:S(2)}, u32[]{:S(2)}) %collective-permute-start.13) | collective-permute-done | bytes 81952 | tf_op jit(solution)/shard_map/ppermute | solution.py:287
  39.9 0.0 collective-permute-done.14.refs_5_
  39.9 0.0 collective-permute-done.15.refs_6_
  39.9 0.0 copy-done
  39.9 0.0 copy-done.1
  39.9 1.0 %unpack.1 = (bf16[128,512]{1,0:T(8,128)(2,1)}, bf16[128,512]{1,0:T(8,128)(2,1)}, bf16[128,512]{1,0:T(8,128)(2,1)}, f32[128,256]{1,0:T(8,128)}) custom-call(f32[160,128]{1,0:T(8,128)S(1)} %collective-permute-done.9.refs_0_, f32[160,128]{1,0:T(8,128)S(1)} %collective-permute-done.10.refs_1_, f32[160,128]{1,0:T(8,128)S(1)} %collective-permute-done.11.refs_2_, ...), custom_call_target="tpu_custom_call" | custom-call | tf_op jit(solution)/shard_map/unpack/pallas_call | solution.py:299
  (1 shorter events, 0.0 us)
Async XLA Ops:
  2.0 11.0 %collective-permute-start = (f32[160,128]{1,0:T(8,128)S(1)}, f32[160,128]{1,0:T(8,128)S(1)}, u32[]{:S(2)}, u32[]{:S(2)}) collective-permute-start(f32[160,128]{1,0:T(8,128)S(1)} %get-tuple-element.31), channel_id=1, source_target_pairs={{0,8},{2,10},{4,12},{6,14},{8,0},{10,2},{12,4},{14,6},{1,9},{3,11}... | collective-permute-start | bytes 245768 | tf_op jit(solution)/shard_map/ppermute | solution.py:287
  6.1 8.7 %collective-permute-start.1 = (f32[160,128]{1,0:T(8,128)S(1)}, f32[160,128]{1,0:T(8,128)S(1)}, u32[]{:S(2)}, u32[]{:S(2)}) collective-permute-start(f32[160,128]{1,0:T(8,128)S(1)} %get-tuple-element.32), channel_id=1, source_target_pairs={{0,4},{2,6},{4,0},{6,2},{8,12},{10,14},{12,8},{14,10},{1,5},{3,7},... | collective-permute-start | bytes 245768 | tf_op jit(solution)/shard_map/ppermute | solution.py:287
  7.7 10.7 %collective-permute-start.2 = (f32[160,128]{1,0:T(8,128)S(1)}, f32[160,128]{1,0:T(8,128)S(1)}, u32[]{:S(2)}, u32[]{:S(2)}) collective-permute-start(f32[160,128]{1,0:T(8,128)S(1)} %get-tuple-element.33), channel_id=1, source_target_pairs={{0,10},{2,8},{4,14},{6,12},{8,2},{10,0},{12,6},{14,4},{1,11},{3,9}... | collective-permute-start | bytes 245768 | tf_op jit(solution)/shard_map/ppermute | solution.py:287
  9.0 9.4 %collective-permute-start.3 = (f32[160,128]{1,0:T(8,128)S(1)}, f32[160,128]{1,0:T(8,128)S(1)}, u32[]{:S(2)}, u32[]{:S(2)}) collective-permute-start(f32[160,128]{1,0:T(8,128)S(1)} %get-tuple-element.34), channel_id=1, source_target_pairs={{0,14},{2,12},{4,10},{6,8},{8,6},{10,4},{12,2},{14,0},{1,15},{3,13... | collective-permute-start | bytes 245768 | tf_op jit(solution)/shard_map/ppermute | solution.py:287
  11.4 8.2 %collective-permute-start.4 = (f32[160,128]{1,0:T(8,128)S(1)}, f32[160,128]{1,0:T(8,128)S(1)}, u32[]{:S(2)}, u32[]{:S(2)}) collective-permute-start(f32[160,128]{1,0:T(8,128)S(1)} %get-tuple-element.35), channel_id=1, source_target_pairs={{0,6},{2,4},{4,2},{6,0},{8,14},{10,12},{12,10},{14,8},{1,7},{3,5},... | collective-permute-start | bytes 245768 | tf_op jit(solution)/shard_map/ppermute | solution.py:287
  13.1 6.6 %collective-permute-start.5 = (f32[160,128]{1,0:T(8,128)S(1)}, f32[160,128]{1,0:T(8,128)S(1)}, u32[]{:S(2)}, u32[]{:S(2)}) collective-permute-start(f32[160,128]{1,0:T(8,128)S(1)} %get-tuple-element.36), channel_id=1, source_target_pairs={{0,12},{2,14},{4,8},{6,10},{8,4},{10,6},{12,0},{14,2},{1,13},{3,15... | collective-permute-start | bytes 245768 | tf_op jit(solution)/shard_map/ppermute | solution.py:287
  14.8 4.8 %collective-permute-start.6 = (f32[160,128]{1,0:T(8,128)S(1)}, f32[160,128]{1,0:T(8,128)S(1)}, u32[]{:S(2)}, u32[]{:S(2)}) collective-permute-start(f32[160,128]{1,0:T(8,128)S(1)} %get-tuple-element.37), channel_id=1, source_target_pairs={{0,2},{2,0},{4,6},{6,4},{8,10},{10,8},{12,14},{14,12},{1,3},{3,1},... | collective-permute-start | bytes 245768 | tf_op jit(solution)/shard_map/ppermute | solution.py:287
  19.7 1.9 %collective-permute-start.7 = (f32[8,32,128]{2,1,0:T(8,128)S(1)}, f32[8,32,128]{2,1,0:T(8,128)S(1)}, u32[]{:S(2)}, u32[]{:S(2)}) collective-permute-start(f32[8,32,128]{2,1,0:T(8,128)S(1)} %gather.1), channel_id=1, source_target_pairs={{0,1},{1,0},{2,3},{3,2},{4,5},{5,4},{6,7},{7,6},{8,9},{9,8},{10,11... | collective-permute-start | bytes 393224 | tf_op jit(solution)/shard_map/ppermute | solution.py:329
  21.0 1.5 %collective-permute-start.8 = (f32[8,32,128]{2,1,0:T(8,128)S(1)}, f32[8,32,128]{2,1,0:T(8,128)S(1)}, u32[]{:S(2)}, u32[]{:S(2)}) collective-permute-start(f32[8,32,128]{2,1,0:T(8,128)S(1)} %get-tuple-element.45), channel_id=1, source_target_pairs={{0,1},{1,0},{2,3},{3,2},{4,5},{5,4},{6,7},{7,6},{8,9},{9,8},{10,11... | collective-permute-start | bytes 393224 | tf_op jit(solution)/shard_map/ppermute | solution.py:329
  21.6 18.3 %copy-start = (bf16[1,128,512]{2,1,0:T(8,128)(2,1)S(1)}, bf16[1,128,512]{2,1,0:T(8,128)(2,1)}, u32[]{:S(2)}) copy-start(bf16[1,128,512]{2,1,0:T(8,128)(2,1)} %param.5) | copy-start | bytes 393220
  21.6 18.3 %copy-start.1 = (bf16[1,128,512]{2,1,0:T(8,128)(2,1)S(1)}, bf16[1,128,512]{2,1,0:T(8,128)(2,1)}, u32[]{:S(2)}) copy-start(bf16[1,128,512]{2,1,0:T(8,128)(2,1)} %param.7) | copy-start | bytes 393220
  22.6 10.2 %collective-permute-start.9 = (f32[160,128]{1,0:T(8,128)S(1)}, f32[160,128]{1,0:T(8,128)S(1)}, u32[]{:S(2)}, u32[]{:S(2)}) collective-permute-start(f32[160,128]{1,0:T(8,128)S(1)} %get-tuple-element.46), channel_id=1, source_target_pairs={{0,8},{2,10},{4,12},{6,14},{8,0},{10,2},{12,4},{14,6},{1,9},{3,11}... | collective-permute-start | bytes 245768 | tf_op jit(solution)/shard_map/ppermute | solution.py:287
  26.5 8.2 %collective-permute-start.10 = (f32[160,128]{1,0:T(8,128)S(1)}, f32[160,128]{1,0:T(8,128)S(1)}, u32[]{:S(2)}, u32[]{:S(2)}) collective-permute-start(f32[160,128]{1,0:T(8,128)S(1)} %get-tuple-element.47), channel_id=1, source_target_pairs={{0,6},{2,4},{4,2},{6,0},{8,14},{10,12},{12,10},{14,8},{1,7},{3,5},... | collective-permute-start | bytes 245768 | tf_op jit(solution)/shard_map/ppermute | solution.py:287
  26.6 11.5 %collective-permute-start.11 = (f32[160,128]{1,0:T(8,128)S(1)}, f32[160,128]{1,0:T(8,128)S(1)}, u32[]{:S(2)}, u32[]{:S(2)}) collective-permute-start(f32[160,128]{1,0:T(8,128)S(1)} %get-tuple-element.48), channel_id=1, source_target_pairs={{0,10},{2,8},{4,14},{6,12},{8,2},{10,0},{12,6},{14,4},{1,11},{3,9}... | collective-permute-start | bytes 245768 | tf_op jit(solution)/shard_map/ppermute | solution.py:287
  29.4 8.6 %collective-permute-start.12 = (f32[160,128]{1,0:T(8,128)S(1)}, f32[160,128]{1,0:T(8,128)S(1)}, u32[]{:S(2)}, u32[]{:S(2)}) collective-permute-start(f32[160,128]{1,0:T(8,128)S(1)} %get-tuple-element.49), channel_id=1, source_target_pairs={{0,14},{2,12},{4,10},{6,8},{8,6},{10,4},{12,2},{14,0},{1,15},{3,13... | collective-permute-start | bytes 245768 | tf_op jit(solution)/shard_map/ppermute | solution.py:287
  32.8 7.1 %collective-permute-start.13 = (f32[160,128]{1,0:T(8,128)S(1)}, f32[160,128]{1,0:T(8,128)S(1)}, u32[]{:S(2)}, u32[]{:S(2)}) collective-permute-start(f32[160,128]{1,0:T(8,128)S(1)} %get-tuple-element.50), channel_id=1, source_target_pairs={{0,4},{2,6},{4,0},{6,2},{8,12},{10,14},{12,8},{14,10},{1,5},{3,7},... | collective-permute-start | bytes 245768 | tf_op jit(solution)/shard_map/ppermute | solution.py:287
  32.8 7.1 %collective-permute-start.14 = (f32[160,128]{1,0:T(8,128)S(1)}, f32[160,128]{1,0:T(8,128)S(1)}, u32[]{:S(2)}, u32[]{:S(2)}) collective-permute-start(f32[160,128]{1,0:T(8,128)S(1)} %get-tuple-element.51), channel_id=1, source_target_pairs={{0,12},{2,14},{4,8},{6,10},{8,4},{10,6},{12,0},{14,2},{1,13},{3,15... | collective-permute-start | bytes 245768 | tf_op jit(solution)/shard_map/ppermute | solution.py:287
  34.7 5.1 %collective-permute-start.15 = (f32[160,128]{1,0:T(8,128)S(1)}, f32[160,128]{1,0:T(8,128)S(1)}, u32[]{:S(2)}, u32[]{:S(2)}) collective-permute-start(f32[160,128]{1,0:T(8,128)S(1)} %get-tuple-element.52), channel_id=1, source_target_pairs={{0,2},{2,0},{4,6},{6,4},{8,10},{10,8},{12,14},{14,12},{1,3},{3,1},... | collective-permute-start | bytes 245768 | tf_op jit(solution)/shard_map/ppermute | solution.py:287
